TPU v7x, 32 devices: a whole 2x2x4 slice. The times are simulated.
32 devices in a mesh: gx: 4 (over z), gy: 4 (over y, x), gz: 2 (over core).
Axes of the slice: x: 2, y: 2, z: 4, core: 2. Of those that a mesh axis runs over, the one named last changes fastest.
Arguments:
- displacement: float32 [3, 128, 128, 512], P(None, 'gx', 'gy', 'gz'), may hold values from -0.0018 to 0.0018
- applied_strain: float32 [6], replicated, may hold values from -0.0003 to 0.0003
- labels: int32 [128, 128, 512], P('gx', 'gy', 'gz'), may hold values from 0 to 3
- history: float32 [128, 128, 512], P('gx', 'gy', 'gz'), may hold values from 5e-05 to 0.0006
- modulus: float32 [4], replicated, may hold values from 5000 to 60000
- poisson: float32 [4], replicated, may hold values from 0.1 to 0.3
- threshold: float32 [4], replicated, may hold values from 4e-05 to 0.00016
- ductility: float32 [4], replicated, may hold values from 0.6 to 1
- brittleness: float32 [4], replicated, may hold values from 5000 to 20000
- weight: float32 [4], replicated, may hold values from 0.1 to 1
Outputs:
- damage: float32 [128, 128, 512], P('gx', 'gy', 'gz')
- mises: float32 [128, 128, 512], P('gx', 'gy', 'gz')
All inputs are finite; a program needn't handle non-finite values.
Results may differ from a plain program's by a relative error of at most 0.0003.
Values sent between devices are 32-bit elements; how exact they have to be, the bound alone decides.
A program may use at most 64 MiB of HBM per device.

v0:
```python
import math

import jax
import jax.numpy as jnp
from jax import lax
from jax.sharding import PartitionSpec as P

RADIUS = 8


def passed_along(block, axis, distance):
    devices = range(lax.axis_size(axis))
    route = [((i - distance) % len(devices), i) for i in devices]
    return lax.ppermute(block, axis, route)


def padded(cells, sides, width):
    for axis, dim in sides:
        count = lax.axis_size(axis)
        head = lax.slice_in_dim(cells, 0, width, axis=dim)
        tail = lax.slice_in_dim(cells, cells.shape[dim] - width, cells.shape[dim], axis=dim)
        cells = jnp.concatenate(
            [
                lax.ppermute(tail, axis, [(i, (i + 1) % count) for i in range(count)]),
                cells,
                lax.ppermute(head, axis, [((i + 1) % count, i) for i in range(count)]),
            ],
            axis=dim,
        )
    return cells


def pick_phase(labels, table):
    picked = jnp.zeros(labels.shape, table.dtype)
    for which_phase in range(table.shape[0]):
        picked = jnp.where(labels == which_phase, table[which_phase], picked)
    return picked


def pair_sum(field, axis):
    length = field.shape[axis]
    return lax.slice_in_dim(field, 0, length - 1, axis=axis) + lax.slice_in_dim(
        field, 1, length, axis=axis
    )


def difference(extended, along, others):
    length = extended.shape[along]
    result = lax.slice_in_dim(extended, 1, length, axis=along) - lax.slice_in_dim(
        extended, 0, length - 1, axis=along
    )
    for other in others:
        result = pair_sum(result, other)
    return 0.25 * result


def invariants(grad_x, grad_y, grad_z, applied_strain):
    strain_xx = applied_strain[0] + grad_x[0]
    strain_yy = applied_strain[1] + grad_y[1]
    strain_zz = applied_strain[2] + grad_z[2]
    strain_yz = applied_strain[3] + 0.5 * (grad_y[2] + grad_z[1])
    strain_xz = applied_strain[4] + 0.5 * (grad_x[2] + grad_z[0])
    strain_xy = applied_strain[5] + 0.5 * (grad_x[1] + grad_y[0])
    trace_strain = strain_xx + strain_yy + strain_zz
    second_inv = (
        (strain_xx - strain_yy) ** 2 + (strain_yy - strain_zz) ** 2 + (strain_zz - strain_xx) ** 2
    ) / 6.0
    second_inv = second_inv + strain_yz * strain_yz + strain_xz * strain_xz + strain_xy * strain_xy
    return (trace_strain, second_inv)


def equivalent(trace_strain, second_inv, ratio_nu):
    ratio = 10.0
    lateral = (ratio - 1.0) / (1.0 - 2.0 * ratio_nu)
    under = (
        lateral * lateral * trace_strain * trace_strain
        + 12.0 * ratio * second_inv / (1.0 + ratio_nu) ** 2
    )
    return (lateral * trace_strain + jnp.sqrt(under)) / (2.0 * ratio)


def smooth_rimmed(extended, axis, length):
    total = None
    for offset in range(-RADIUS, RADIUS + 1):
        coeff = math.exp(-2.0 * offset * offset / (RADIUS * RADIUS))
        start = offset + RADIUS
        term = coeff * lax.slice_in_dim(extended, start, start + length, axis=axis)
        total = term if total is None else total + term
    return total


def finish(
    averaged, history, second_inv, labels, ratio_nu, modulus, threshold, ductility, brittleness
):
    kappa = jnp.maximum(history, averaged)
    start = pick_phase(labels, threshold)
    ductile = pick_phase(labels, ductility)
    brittle = pick_phase(labels, brittleness)
    grown = (
        1.0
        - start * (1.0 - ductile) / jnp.maximum(kappa, start)
        - ductile * jnp.exp(-brittle * (kappa - start))
    )
    damage = jnp.where(kappa > start, grown, 0.0)
    stiff = pick_phase(labels, modulus)
    mises = (1.0 - damage) * stiff / (1.0 + ratio_nu) * jnp.sqrt(3.0 * second_inv)
    return (damage, mises)


def shards(
    displacement,
    applied_strain,
    labels,
    history,
    modulus,
    poisson,
    threshold,
    ductility,
    brittleness,
    weight,
):
    cells_x, cells_y, cells_z = labels.shape
    plane = passed_along(displacement[:, 0:1], "gx", -1)
    nodes = jnp.concatenate([displacement, plane], axis=1)
    plane = passed_along(nodes[:, :, 0:1], "gy", -1)
    nodes = jnp.concatenate([nodes, plane], axis=2)
    plane = passed_along(nodes[:, :, :, 0:1], "gz", -1)
    nodes = jnp.concatenate([nodes, plane], axis=3)
    grad_x = difference(nodes, 1, (2, 3))
    grad_y = difference(nodes, 2, (1, 3))
    grad_z = difference(nodes, 3, (1, 2))
    trace_strain, second_inv = invariants(grad_x, grad_y, grad_z, applied_strain)
    ratio_nu = pick_phase(labels, poisson)
    equiv_strain = equivalent(trace_strain, second_inv, ratio_nu)
    weights_field = pick_phase(labels, weight)
    stacked = jnp.stack([weights_field * equiv_strain, weights_field])
    rimmed = padded(stacked, (("gx", 1),), RADIUS)
    smoothed = smooth_rimmed(rimmed, 1, cells_x)
    rimmed = padded(smoothed, (("gy", 2),), RADIUS)
    smoothed = smooth_rimmed(rimmed, 2, cells_y)
    rimmed = padded(smoothed, (("gz", 3),), RADIUS)
    smoothed = smooth_rimmed(rimmed, 3, cells_z)
    averaged = smoothed[0] / smoothed[1]
    return finish(
        averaged, history, second_inv, labels, ratio_nu, modulus, threshold, ductility, brittleness
    )


def solution(mesh):
    placed = (
        P(None, "gx", "gy", "gz"),
        P(),
        P("gx", "gy", "gz"),
        P("gx", "gy", "gz"),
        P(),
        P(),
        P(),
        P(),
        P(),
        P(),
    )
    return jax.shard_map(
        shards,
        mesh=mesh,
        in_specs=placed,
        out_specs=(P("gx", "gy", "gz"), P("gx", "gy", "gz")),
        check_vma=False,
    )
```

profile of v0, /device:TPU:0, one launch (start us, length us, event | category | flops | bytes accessed | tf_op | source)
XLA Modules:
  0.0 154.8 jit_solution(1145243454611955699)
XLA Ops:
  1.6 5.1 %collective-permute-start = (f32[3,1,32,256]{3,2,1,0:T(8,128)S(1)}, f32[3,1,32,256]{3,2,1,0:T(8,128)S(1)}, u32[]{:S(2)}, u32[]{:S(2)}) collective-permute-start(f32[3,1,32,256]{3,2,1,0:T(8,128)S(1)} %slice.402), channel_id=1, source_target_pairs={{8,0},{16,8},{24,16},{0,24},{9,1},{17,9},{25,17},{1,25},{10,2},{18... | collective-permute-start | bytes 294920 | tf_op jit(solution)/shard_map/ppermute | solution.py:14
  6.7 2.1 %constant_dynamic-update-slice_fusion.1 = f32[3,33,32,256]{3,2,1,0:T(8,128)S(1)} fusion(f32[3,32,32,256]{3,2,1,0:T(8,128)} %param.10), kind=kLoop, calls=%fused_computation.256 | loop fusion | bytes 6291456
  9.6 2.5 %collective-permute-start.1 = (f32[3,33,1,256]{3,2,1,0:T(1,128)S(1)}, f32[3,33,1,256]{3,2,1,0:T(1,128)S(1)}, u32[]{:S(2)}, u32[]{:S(2)}) collective-permute-start(f32[3,33,1,256]{3,2,1,0:T(1,128)S(1)} %slice.508), channel_id=1, source_target_pairs={{2,0},{4,2},{6,4},{0,6},{3,1},{5,3},{7,5},{1,7},{10,8},{12,10},{14... | collective-permute-start | bytes 304136 | tf_op jit(solution)/shard_map/ppermute | solution.py:14
  12.7 1.6 %collective-permute-done.1 = f32[3,33,1,256]{3,2,1,0:T(1,128)S(1)} collective-permute-done((f32[3,33,1,256]{3,2,1,0:T(1,128)S(1)}, f32[3,33,1,256]{3,2,1,0:T(1,128)S(1)}, u32[]{:S(2)}, u32[]{:S(2)}) %collective-permute-start.1) | collective-permute-done | bytes 101408 | tf_op jit(solution)/shard_map/ppermute | solution.py:14
  14.3 1.5 fusion.112
  15.8 2.3 %copy.27 = f32[3,33,33,1]{2,3,1,0:T(1,128)S(1)} copy(f32[3,33,33,1]{3,2,1,0:T(8,128)} %fusion.112) | data formatting | bytes 26136
  19.5 2.2 %copy.22 = f32[3,33,33,1]{3,2,1,0:T(8,128)} copy(f32[3,33,33,1]{2,3,1,0:T(1,128)S(1)} %collective-permute-done.2) | data formatting | bytes 26136 | tf_op jit(solution)/shard_map/ppermute | solution.py:14
  21.6 2.0 %pad_maximum_fusion = f32[3,33,33,257]{3,2,1,0:T(8,128)S(1)} fusion(f32[3,33,33,1]{3,2,1,0:T(8,128)} %copy.22, f32[3,33,1,256]{3,2,1,0:T(1,128)S(1)} %collective-permute-done.1, f32[3,33,32,256]{3,2,1,0:T(8,128)S(1)} %constant_dynamic-update-slice_fusion), kind=kLoop, calls=%fused_computation.28 | loop fusion | flops 1679238 | bytes 6716952 | tf_op jit(solution)/shard_map/concatenate | solution.py:128
  25.7 2.5 %fusion.3 = f32[3,32,32,256]{3,2,1,0:T(8,128)} fusion(f32[3,32,32,257]{3,2,1,0:T(8,128)S(1)} %slice_add_fusion.1), kind=kLoop, calls=%fused_computation.71 | loop fusion | flops 1572864 | bytes 9437184 | tf_op jit(solution)/shard_map/mul | solution.py:54
  30.3 3.0 %fusion.1 = (f32[3,32,32,256]{3,2,1,0:T(8,128)S(1)}, f32[3,32,32,256]{3,2,1,0:T(8,128)}) fusion(f32[3,32,33,256]{3,2,1,0:T(8,128)S(1)} %slice_add_fusion.2, f32[3,32,32,257]{3,2,1,0:T(8,128)S(1)} %slice_add_fusion), kind=kLoop, calls=%fused_computation.67 | loop fusion | flops 3145728 | bytes 18874368 | tf_op jit(solution)/shard_map/mul | solution.py:54
  33.3 14.0 %fusion.118 = (f32[1,32,32,256]{3,2,1,0:T(8,128)S(1)}, f32[32,32,256]{2,1,0:T(8,128)}, pred[32,32,256]{2,1,0:T(8,128)(4,1)S(1)}, pred[32,32,256]{2,1,0:T(8,128)(...) fusion(f32[3,32,32,256]{3,2,1,0:T(8,128)} %fusion.3, ...), kind=kLoop, calls=%fused_computation.214 | loop fusion | flops 14680064 | bytes 13631544 | tf_op jit(solution)/shard_map/stack | solution.py:136
  47.4 2.9 %fusion.140 = f32[1,32,32,256]{3,2,1,0:T(8,128)S(1)} fusion(pred[32,32,256]{2,1,0:T(8,128)(4,1)S(1)} %get-tuple-element.11, pred[32,32,256]{2,1,0:T(8,128)(4,1)S(1)} %get-tuple-element.10, pred[32,32,256]{2,1,0:T(8,128)(4,1)S(1)} %get-tuple-element.9, pred[32,32,256]{2,1,0:T(8,128)(4,1)S(1)} %get-tuple-element.8, f32[]{:T(128)} %bitcast.3, f32[]{:T(128)} %bitcast.2, ...), kind=kLoop, calls=%fused_computation.248 | loop fusion | flops 1048576 | bytes 2097168 | tf_op jit(solution)/shard_map/stack | solution.py:136
  50.5 3.8 %collective-permute-start.4 = (f32[2,8,32,256]{3,2,1,0:T(8,128)S(1)}, f32[2,8,32,256]{3,2,1,0:T(8,128)S(1)}, u32[]{:S(2)}, u32[]{:S(2)}) collective-permute-start(f32[2,8,32,256]{3,2,1,0:T(8,128)S(1)} %get-tuple-element.19), channel_id=1, source_target_pairs={{8,0},{16,8},{24,16},{0,24},{9,1},{17,9},{25,17},{1,25},{10,2},{18... | collective-permute-start | bytes 1572872 | tf_op jit(solution)/shard_map/ppermute | solution.py:26
  54.3 12.8 %collective-permute-done.3 = f32[2,8,32,256]{3,2,1,0:T(8,128)S(1)} collective-permute-done((f32[2,8,32,256]{3,2,1,0:T(8,128)S(1)}, f32[2,8,32,256]{3,2,1,0:T(8,128)S(1)}, u32[]{:S(2)}, u32[]{:S(2)}) %collective-permute-start.3) | collective-permute-done | bytes 524320 | tf_op jit(solution)/shard_map/ppermute | solution.py:24
  67.1 8.9 %collective-permute-done.4 = f32[2,8,32,256]{3,2,1,0:T(8,128)S(1)} collective-permute-done((f32[2,8,32,256]{3,2,1,0:T(8,128)S(1)}, f32[2,8,32,256]{3,2,1,0:T(8,128)S(1)}, u32[]{:S(2)}, u32[]{:S(2)}) %collective-permute-start.4) | collective-permute-done | bytes 524320 | tf_op jit(solution)/shard_map/ppermute | solution.py:26
  76.8 4.7 %fusion.12 = f32[2,32,32,256]{3,2,1,0:T(8,128)S(1)} fusion(f32[1,32,32,256]{3,2,1,0:T(8,128)S(1)} %fusion.140, f32[1,32,32,256]{3,2,1,0:T(8,128)S(1)} %get-tuple-element.6, f32[2,40,32,256]{3,2,1,0:T(8,128)S(1)} %get-tuple-element.17, f32[2,40,32,256]{3,2,1,0:T(8,128)S(1)} %get-tuple-element.16), kind=kLoop, calls=%fused_computation.87 | loop fusion | flops 17301504 | bytes 37748736 | tf_op jit(solution)/shard_map/add | solution.py:88
  81.6 3.4 %collective-permute-start.6 = (f32[2,32,8,256]{3,2,1,0:T(8,128)S(1)}, f32[2,32,8,256]{3,2,1,0:T(8,128)S(1)}, u32[]{:S(2)}, u32[]{:S(2)}) collective-permute-start(f32[2,32,8,256]{3,2,1,0:T(8,128)S(1)} %get-tuple-element.15), channel_id=1, source_target_pairs={{2,0},{4,2},{6,4},{0,6},{3,1},{5,3},{7,5},{1,7},{10,8},{12,10},{14... | collective-permute-start | bytes 1572872 | tf_op jit(solution)/shard_map/ppermute | solution.py:26
  86.9 10.4 %collective-permute-done.6 = f32[2,32,8,256]{3,2,1,0:T(8,128)S(1)} collective-permute-done((f32[2,32,8,256]{3,2,1,0:T(8,128)S(1)}, f32[2,32,8,256]{3,2,1,0:T(8,128)S(1)}, u32[]{:S(2)}, u32[]{:S(2)}) %collective-permute-start.6) | collective-permute-done | bytes 524320 | tf_op jit(solution)/shard_map/ppermute | solution.py:26
  97.3 10.3 %collective-permute-done.5 = f32[2,32,8,256]{3,2,1,0:T(8,128)S(1)} collective-permute-done((f32[2,32,8,256]{3,2,1,0:T(8,128)S(1)}, f32[2,32,8,256]{3,2,1,0:T(8,128)S(1)}, u32[]{:S(2)}, u32[]{:S(2)}) %collective-permute-start.5) | collective-permute-done | bytes 524320 | tf_op jit(solution)/shard_map/ppermute | solution.py:24
  107.6 5.2 %fusion.16 = f32[2,32,32,256]{3,2,1,0:T(8,128)S(1)} fusion(f32[2,32,32,256]{3,2,1,0:T(8,128)S(1)} %fusion.12, f32[2,32,8,256]{3,2,1,0:T(8,128)S(1)} %collective-permute-done.6, f32[2,32,8,256]{3,2,1,0:T(8,128)S(1)} %collective-permute-done.5), kind=kLoop, calls=%fused_computation.91 | loop fusion | flops 25165824 | bytes 5242880 | tf_op jit(solution)/shard_map/add | solution.py:88
  114.2 2.3 %copy.25 = f32[2,32,32,8]{2,3,1,0:T(8,128)} copy(f32[2,32,32,8]{3,2,1,0:T(8,128)} %get-tuple-element.13) | data formatting | bytes 131072 | tf_op jit(solution)/shard_map/slice | solution.py:20
  119.9 2.3 %copy.24 = f32[2,32,32,8]{3,2,1,0:T(8,128)} copy(f32[2,32,32,8]{2,3,1,0:T(8,128)} %collective-permute-done.7) | data formatting | bytes 131072 | tf_op jit(solution)/shard_map/ppermute | solution.py:24
  122.3 16.9 %fusion.60 = f32[2,32,32,256]{3,2,1,0:T(8,128)S(1)} fusion(f32[2,32,32,256]{3,2,1,0:T(8,128)S(1)} %fusion.16, f32[2,32,32,8]{3,2,1,0:T(8,128)S(1)} %copy.26, f32[2,32,32,8]{3,2,1,0:T(8,128)} %copy.24), kind=kLoop, calls=%fused_computation.135 | loop fusion | flops 25165824 | bytes 4325376 | tf_op jit(solution)/shard_map/add | solution.py:88
  139.2 15.6 %sqrt_multiply_fusion = (f32[32,32,256]{2,1,0:T(8,128)}, f32[32,32,256]{2,1,0:T(8,128)}) fusion(f32[32,32,256]{2,1,0:T(8,128)S(1)} %copy-done, pred[32,32,256]{2,1,0:T(8,128)(4,1)S(1)} %copy-done.6, pred[32,32,256]{2,1,0:T(8,128)(4,1)S(1)} %copy-done.4, pred[32,32,256]{2,1,0:T(8,128)(4,1)S(1)} %copy-done.2, pred[32,32,256]{2,1,0:T(8,128)(4,1)S(1)} %get-tuple-element.8, ...), kind=kLoop, calls=%fused_computation.242 | loop fusion | flops 10485760 | bytes 7340112 | tf_op jit(solution)/shard_map/mul | solution.py:106
  (63 shorter events, 15.7 us)
Async XLA Ops:
  1.5 7.2 %copy-start.9 = (f32[6]{0:T(128)S(1)}, f32[6]{0:T(128)}, u32[]{:S(2)}) copy-start(f32[6]{0:T(128)} %param.11) | copy-start | bytes 76
  1.5 10.5 %copy-start.10 = (f32[4]{0:T(128)S(1)}, f32[4]{0:T(128)}, u32[]{:S(2)}) copy-start(f32[4]{0:T(128)} %param.15) | copy-start | bytes 52
  1.6 7.9 %collective-permute-start = (f32[3,1,32,256]{3,2,1,0:T(8,128)S(1)}, f32[3,1,32,256]{3,2,1,0:T(8,128)S(1)}, u32[]{:S(2)}, u32[]{:S(2)}) collective-permute-start(f32[3,1,32,256]{3,2,1,0:T(8,128)S(1)} %slice.402), channel_id=1, source_target_pairs={{8,0},{16,8},{24,16},{0,24},{9,1},{17,9},{25,17},{1,25},{10,2},{18... | collective-permute-start | bytes 294920 | tf_op jit(solution)/shard_map/ppermute | solution.py:14
  9.6 4.7 %collective-permute-start.1 = (f32[3,33,1,256]{3,2,1,0:T(1,128)S(1)}, f32[3,33,1,256]{3,2,1,0:T(1,128)S(1)}, u32[]{:S(2)}, u32[]{:S(2)}) collective-permute-start(f32[3,33,1,256]{3,2,1,0:T(1,128)S(1)} %slice.508), channel_id=1, source_target_pairs={{2,0},{4,2},{6,4},{0,6},{3,1},{5,3},{7,5},{1,7},{10,8},{12,10},{14... | collective-permute-start | bytes 304136 | tf_op jit(solution)/shard_map/ppermute | solution.py:14
  12.7 5.6 %copy-start.11 = (f32[4]{0:T(128)S(1)}, f32[4]{0:T(128)}, u32[]{:S(2)}) copy-start(f32[4]{0:T(128)} %param.19) | copy-start | bytes 52
  18.2 1.3 collective-permute-start.2
  47.3 3.0 %copy-start.1 = (pred[32,32,256]{2,1,0:T(8,128)(4,1)}, pred[32,32,256]{2,1,0:T(8,128)(4,1)S(1)}, u32[]{:S(2)}) copy-start(pred[32,32,256]{2,1,0:T(8,128)(4,1)S(1)} %get-tuple-element.9) | copy-start | bytes 786436
  47.3 3.1 %copy-start.3 = (pred[32,32,256]{2,1,0:T(8,128)(4,1)}, pred[32,32,256]{2,1,0:T(8,128)(4,1)S(1)}, u32[]{:S(2)}) copy-start(pred[32,32,256]{2,1,0:T(8,128)(4,1)S(1)} %get-tuple-element.10) | copy-start | bytes 786436
  47.3 3.1 %copy-start.5 = (pred[32,32,256]{2,1,0:T(8,128)(4,1)}, pred[32,32,256]{2,1,0:T(8,128)(4,1)S(1)}, u32[]{:S(2)}) copy-start(pred[32,32,256]{2,1,0:T(8,128)(4,1)S(1)} %get-tuple-element.11) | copy-start | bytes 786436
  50.4 16.7 %collective-permute-start.3 = (f32[2,8,32,256]{3,2,1,0:T(8,128)S(1)}, f32[2,8,32,256]{3,2,1,0:T(8,128)S(1)}, u32[]{:S(2)}, u32[]{:S(2)}) collective-permute-start(f32[2,8,32,256]{3,2,1,0:T(8,128)S(1)} %get-tuple-element.18), channel_id=1, source_target_pairs={{0,8},{8,16},{16,24},{24,0},{1,9},{9,17},{17,25},{25,1},{2,10},{10... | collective-permute-start | bytes 1572872 | tf_op jit(solution)/shard_map/ppermute | solution.py:24
  50.5 25.5 %collective-permute-start.4 = (f32[2,8,32,256]{3,2,1,0:T(8,128)S(1)}, f32[2,8,32,256]{3,2,1,0:T(8,128)S(1)}, u32[]{:S(2)}, u32[]{:S(2)}) collective-permute-start(f32[2,8,32,256]{3,2,1,0:T(8,128)S(1)} %get-tuple-element.19), channel_id=1, source_target_pairs={{8,0},{16,8},{24,16},{0,24},{9,1},{17,9},{25,17},{1,25},{10,2},{18... | collective-permute-start | bytes 1572872 | tf_op jit(solution)/shard_map/ppermute | solution.py:26
  81.4 3.5 %copy-start.12 = (f32[4]{0:T(128)S(1)}, f32[4]{0:T(128)}, u32[]{:S(2)}) copy-start(f32[4]{0:T(128)} %param.14) | copy-start | bytes 52
  81.4 4.2 %copy-start.13 = (f32[4]{0:T(128)S(1)}, f32[4]{0:T(128)}, u32[]{:S(2)}) copy-start(f32[4]{0:T(128)} %param.18) | copy-start | bytes 52
  81.4 4.8 %copy-start.14 = (f32[4]{0:T(128)S(1)}, f32[4]{0:T(128)}, u32[]{:S(2)}) copy-start(f32[4]{0:T(128)} %param.17) | copy-start | bytes 52
  81.6 15.7 %collective-permute-start.6 = (f32[2,32,8,256]{3,2,1,0:T(8,128)S(1)}, f32[2,32,8,256]{3,2,1,0:T(8,128)S(1)}, u32[]{:S(2)}, u32[]{:S(2)}) collective-permute-start(f32[2,32,8,256]{3,2,1,0:T(8,128)S(1)} %get-tuple-element.15), channel_id=1, source_target_pairs={{2,0},{4,2},{6,4},{0,6},{3,1},{5,3},{7,5},{1,7},{10,8},{12,10},{14... | collective-permute-start | bytes 1572872 | tf_op jit(solution)/shard_map/ppermute | solution.py:26
  84.9 22.7 %collective-permute-start.5 = (f32[2,32,8,256]{3,2,1,0:T(8,128)S(1)}, f32[2,32,8,256]{3,2,1,0:T(8,128)S(1)}, u32[]{:S(2)}, u32[]{:S(2)}) collective-permute-start(f32[2,32,8,256]{3,2,1,0:T(8,128)S(1)} %get-tuple-element.14), channel_id=1, source_target_pairs={{0,2},{2,4},{4,6},{6,0},{1,3},{3,5},{5,7},{7,1},{8,10},{10,12},{12... | collective-permute-start | bytes 1572872 | tf_op jit(solution)/shard_map/ppermute | solution.py:24
  114.2 3.8 %copy-start.15 = (f32[4]{0:T(128)S(1)}, f32[4]{0:T(128)}, u32[]{:S(2)}) copy-start(f32[4]{0:T(128)} %param.16) | copy-start | bytes 52
  116.4 2.2 %collective-permute-start.8 = (f32[2,32,32,8]{2,3,1,0:T(8,128)}, f32[2,32,32,8]{2,3,1,0:T(8,128)}, u32[]{:S(2)}, u32[]{:S(2)}) collective-permute-start(f32[2,32,32,8]{2,3,1,0:T(8,128)} %copy.25), channel_id=1, source_target_pairs={{1,0},{0,1},{3,2},{2,3},{5,4},{4,5},{7,6},{6,7},{9,8},{8,9},{11,10... | collective-permute-start | bytes 196616 | tf_op jit(solution)/shard_map/ppermute | solution.py:26
  117.5 2.5 %collective-permute-start.7 = (f32[2,32,32,8]{2,3,1,0:T(8,128)}, f32[2,32,32,8]{2,3,1,0:T(8,128)}, u32[]{:S(2)}, u32[]{:S(2)}) collective-permute-start(f32[2,32,32,8]{2,3,1,0:T(8,128)} %copy.23), channel_id=1, source_target_pairs={{0,1},{1,0},{2,3},{3,2},{4,5},{5,4},{6,7},{7,6},{8,9},{9,8},{10,11... | collective-permute-start | bytes 196616 | tf_op jit(solution)/shard_map/ppermute | solution.py:24
  122.2 16.9 %copy-start = (f32[32,32,256]{2,1,0:T(8,128)S(1)}, f32[32,32,256]{2,1,0:T(8,128)}, u32[]{:S(2)}) copy-start(f32[32,32,256]{2,1,0:T(8,128)} %get-tuple-element.7) | copy-start | bytes 3145732
  122.2 17.0 %copy-start.2 = (pred[32,32,256]{2,1,0:T(8,128)(4,1)S(1)}, pred[32,32,256]{2,1,0:T(8,128)(4,1)}, u32[]{:S(2)}) copy-start(pred[32,32,256]{2,1,0:T(8,128)(4,1)} %copy-done.1) | copy-start | bytes 786436
  122.2 17.0 %copy-start.4 = (pred[32,32,256]{2,1,0:T(8,128)(4,1)S(1)}, pred[32,32,256]{2,1,0:T(8,128)(4,1)}, u32[]{:S(2)}) copy-start(pred[32,32,256]{2,1,0:T(8,128)(4,1)} %copy-done.3) | copy-start | bytes 786436
  122.2 17.0 %copy-start.6 = (pred[32,32,256]{2,1,0:T(8,128)(4,1)S(1)}, pred[32,32,256]{2,1,0:T(8,128)(4,1)}, u32[]{:S(2)}) copy-start(pred[32,32,256]{2,1,0:T(8,128)(4,1)} %copy-done.5) | copy-start | bytes 786436
  122.2 17.0 %copy-start.7 = (f32[32,32,256]{2,1,0:T(8,128)S(1)}, f32[32,32,256]{2,1,0:T(8,128)}, u32[]{:S(2)}) copy-start(f32[32,32,256]{2,1,0:T(8,128)} %param.13) | copy-start | bytes 3145732
  (1 other events, 3.0 us)
where the time goes:
time: 156 us; the launch traced here: 155 us
  other arithmetic  73.4 us (47%)
  waiting for transfers between devices  44.4 us (28%)
  local copies, waits for them, and re-layouts  20.6 us (13%)
  starting transfers between devices  15.4 us (10%)
    add x3, other arithmetic, smooth_rimmed(): total = term if total is None else total + term  26.8 us
    ppermute x3, waiting for transfers between devices, padded(): lax.ppermute(tail, axis, [(i, (i + 1) % count) for i in range(count)])  23 us
    ppermute x3, waiting for transfers between devices, padded(): lax.ppermute(head, axis, [((i + 1) % count, i) for i in range(count)])  19.2 us
    another operation x3, other arithmetic, shards(): stacked = jnp.stack([weights_field * equiv_strain, weights_field])  17 us
    mul x1, other arithmetic, finish(): (1.0 - damage) * stiff / (1.0 + ratio_nu) * jnp.sqrt(3.0 * second_inv)  15.6 us
    ppermute x3, starting transfers between devices, passed_along(): return lax.ppermute(block, axis, route)  7.67 us
    ppermute x3, starting transfers between devices, padded(): lax.ppermute(head, axis, [((i + 1) % count, i) for i in range(count)])  7.19 us
    mul x2, other arithmetic, difference(): return 0.25 * result  5.51 us
  transfers between devices with their start and end apart: 9, of which 6 were waited for; matrix products, arithmetic and copies ran while one was open for 6% of the time, Pallas kernels for 0%

commit v1 on v0

v1 whole, which is shorter than its diff:
```python
import functools
import math

import jax
import jax.numpy as jnp
from jax import lax
from jax.experimental import pallas as pl
from jax.experimental.pallas import tpu as pltpu
from jax.sharding import PartitionSpec as P

RADIUS = 8
LANES = 128
ROWS = 8
MESH = pl.DeviceIdType.MESH
TAPS = [math.exp(-2.0 * s * s / (RADIUS * RADIUS)) for s in range(RADIUS + 1)]
T_WEIGHT, T_LATERAL, T_FACTOR, T_WEIGHT_EQ, T_START, T_LOSS, T_DUCTILE, T_BRITTLE, T_STIFF = range(9)


def phase_masks(labels):
    return (labels == 0, labels == 1, labels == 2)


def pick(masks, tab, which):
    rows = [tab[pl.ds(4 * which + p, 1), : masks[0].shape[-1]] for p in range(4)]
    return jnp.where(
        masks[0], rows[0], jnp.where(masks[1], rows[1], jnp.where(masks[2], rows[2], rows[3]))
    )


def fill_tables(tab, modulus, poisson, threshold, ductility, brittleness, weight):
    width = tab.shape[-1]

    def put(which, phase, value):
        tab[4 * which + phase : 4 * which + phase + 1, :] = value

    for p in range(4):
        wide = lambda ref: jnp.full((1, width), ref[p], jnp.float32)
        nu, start, ductile, w = wide(poisson), wide(threshold), wide(ductility), wide(weight)
        put(T_WEIGHT, p, w)
        put(T_LATERAL, p, 9.0 / (1.0 - 2.0 * nu))
        put(T_FACTOR, p, 120.0 / ((1.0 + nu) * (1.0 + nu)))
        put(T_WEIGHT_EQ, p, w * 0.05)
        put(T_START, p, start)
        put(T_LOSS, p, start * (1.0 - ductile))
        put(T_DUCTILE, p, ductile)
        put(T_BRITTLE, p, -wide(brittleness))
        put(T_STIFF, p, wide(modulus) / (1.0 + nu) * math.sqrt(3.0))


def fill_bands(band_hi, band_lo):
    depth, width = band_hi.shape

    @pl.loop(0, depth // LANES)
    def _(i):
        rows = pl.ds(pl.multiple_of(i * LANES, LANES), LANES)
        k = lax.broadcasted_iota(jnp.int32, (LANES, width), 0) + i * LANES
        n = lax.broadcasted_iota(jnp.int32, (LANES, width), 1)
        d = (k - LANES - n).astype(jnp.float32)
        g = jnp.where(jnp.abs(d) <= RADIUS, jnp.exp(d * d * (-2.0 / (RADIUS * RADIUS))), 0.0)
        hi = g.astype(jnp.bfloat16)
        band_hi[rows, :] = hi
        band_lo[rows, :] = (g - hi.astype(jnp.float32)).astype(jnp.bfloat16)


def smooth_x(src, first, count):
    col = [src(first + i) for i in range(count + 2 * RADIUS)]
    outs = []
    for i in range(count):
        total = TAPS[0] * col[i + RADIUS]
        for s in range(1, RADIUS + 1):
            total = total + TAPS[s] * (col[i + RADIUS - s] + col[i + RADIUS + s])
        outs.append(total)
    return outs


def smooth_x_into(src, put, cells_x, cells_y):
    @pl.loop(0, cells_x // 8)
    def _(i):
        @pl.loop(0, cells_y // ROWS)
        def _(j):
            rows = pl.ds(pl.multiple_of(j * ROWS, ROWS), ROWS)
            outs = smooth_x(lambda x: src[i * 8 + x, rows, :], 0, 8)
            for x, value in enumerate(outs):
                put(i * 8 + x, rows, value)


def smooth_y(block):
    long = block.shape[0] - ROWS
    cells_y = block.shape[0] - 2 * RADIUS
    total = None
    for r in range(ROWS):
        part = None
        for q in range(3):
            s = ROWS * q + r
            if s > 2 * RADIUS:
                continue
            rows = cells_y if r == 0 else long
            term = TAPS[abs(s - RADIUS)] * block[ROWS * q : ROWS * q + rows]
            part = term if part is None else part + term
        if r:
            part = pltpu.roll(part, long - r, 0)[:cells_y]
        total = part if total is None else total + part
    return total


def smooth_z(planes, left, own, right, band_hi, band_lo):
    depth = band_hi.shape[0]
    cells_y = own.shape[1]
    rows = planes.size * cells_y
    block = jnp.concatenate([left[planes], own[planes], right[planes]], axis=2)
    block = block.reshape(rows, depth)
    hi = block.astype(jnp.bfloat16)
    lo = (block - hi.astype(jnp.float32)).astype(jnp.bfloat16)
    dot = functools.partial(jnp.dot, preferred_element_type=jnp.float32)
    out = dot(lo, band_hi[...]) + dot(hi, band_lo[...]) + dot(hi, band_hi[...])
    return out.reshape(planes.size, cells_y, out.shape[-1])


def kernel(
    disp, labels, history, strain0, modulus, poisson, threshold, ductility, brittleness, weight,
    damage_out, mises_out,
    ext, ysend, ybuf, ebuf, lab, hist, second, traw, tab, band_hi, band_lo,
    w_ax, w_ay, w_by, w_bx, t_ax, t_ay, t_by, t_bx,
    wfull, wl, wr, tl, tr, damage_v, mises_v,
    in_sem, out_sem, send_sem, recv_sem,
):
    cells_x, cells_y, cells_z = labels.shape
    half = cells_z // 2
    names = ("gx", "gy", "gz")
    count = {a: lax.axis_size(a) for a in names}
    here = {a: lax.axis_index(a) for a in names}

    def at(**moved):
        return tuple(lax.rem(here[a] + moved.get(a, 0) + count[a], count[a]) for a in names)

    x_up, x_down, y_up, y_down = at(gx=1), at(gx=-1), at(gy=1), at(gy=-1)
    z_up, z_down, d_up, d_down = at(gz=1), at(gz=-1), at(gx=1, gy=1), at(gx=-1, gy=-1)

    load_lab = pltpu.make_async_copy(labels, lab, in_sem.at[0])
    load_disp = pltpu.make_async_copy(
        disp, ext.at[:, pl.ds(0, cells_x), pl.ds(0, cells_y), pl.ds(0, cells_z)], in_sem.at[1]
    )
    load_hist = pltpu.make_async_copy(history, hist, in_sem.at[2])
    load_lab.start()
    load_disp.start()
    load_hist.start()

    barrier = pltpu.get_barrier_semaphore()
    greeted = (x_up, x_down, y_up, y_down, z_up, z_down, d_up, d_down)
    for device in greeted:
        pl.semaphore_signal(barrier, inc=1, device_id=device, device_id_type=MESH)

    slots = iter(range(send_sem.shape[0]))

    def remote(src, dst, device):
        slot = next(slots)
        copy = pltpu.make_async_remote_copy(
            src_ref=src, dst_ref=dst, send_sem=send_sem.at[slot], recv_sem=recv_sem.at[slot],
            device_id=device, device_id_type=MESH,
        )
        copy.start()
        return copy

    def halo_x(buf):
        return (
            remote(buf.at[pl.ds(RADIUS, RADIUS)], buf.at[pl.ds(cells_x + RADIUS, RADIUS)], x_down),
            remote(buf.at[pl.ds(cells_x, RADIUS)], buf.at[pl.ds(0, RADIUS)], x_up),
        )

    def halo_y(buf):
        return (
            remote(
                buf.at[:, pl.ds(RADIUS, RADIUS)], buf.at[:, pl.ds(cells_y + RADIUS, RADIUS)], y_down
            ),
            remote(buf.at[:, pl.ds(cells_y, RADIUS)], buf.at[:, pl.ds(0, RADIUS)], y_up),
        )

    def halo_z(buf, left, right):
        return (
            remote(buf.at[:, :, pl.ds(0, LANES)], right, z_down),
            remote(buf.at[:, :, pl.ds(cells_z - LANES, LANES)], left, z_up),
        )

    fill_tables(tab, modulus, poisson, threshold, ductility, brittleness, weight)
    load_lab.wait()

    @pl.loop(0, cells_x)
    def _(x):
        w = pick(phase_masks(lab[x]), tab, T_WEIGHT)
        w_ax[x + RADIUS] = w[:, :half]
        w_by[x, RADIUS : RADIUS + cells_y, :] = w[:, half:]

    load_disp.wait()

    @pl.loop(0, cells_x)
    def _(x):
        for c in range(3):
            ysend[c, pl.ds(x, 1), :] = ext[c, x, 0:1, :cells_z]

    pl.semaphore_wait(barrier, len(greeted))

    zcols = pl.ds(cells_z, LANES)
    first = pl.ds(0, LANES)
    ys = pl.ds(0, cells_y)
    node_x = remote(disp.at[:, 0], ext.at[:, cells_x, ys, pl.ds(0, cells_z)], x_down)
    node_y = remote(ysend, ybuf.at[:, :, pl.ds(0, cells_z)], y_down)
    node_e = remote(disp.at[:, 0, pl.ds(0, ROWS)], ebuf.at[:, :, pl.ds(0, cells_z)], d_down)
    node_z = remote(
        disp.at[:, :, :, first], ext.at[:, pl.ds(0, cells_x), ys, zcols], z_down
    )
    w1 = halo_x(w_ax) + halo_y(w_by)
    fill_bands(band_hi, band_lo)
    node_x.wait_recv()
    node_zx = remote(ext.at[:, cells_x, ys, first], ext.at[:, cells_x, ys, zcols], z_down)
    node_e.wait_recv()
    node_ze = remote(ebuf.at[:, :, first], ebuf.at[:, :, zcols], z_down)
    node_y.wait_recv()
    node_zy = remote(ybuf.at[:, :, first], ybuf.at[:, :, zcols], z_down)
    for copy in (node_z, node_zx, node_ze, node_zy):
        copy.wait_recv()

    wide = ext.shape[3]

    @pl.loop(0, cells_x)
    def _(x):
        for c in range(3):
            ext[c, x, cells_y : cells_y + ROWS, :] = jnp.broadcast_to(
                ybuf[c, pl.ds(x, 1), :], (ROWS, wide)
            )

    for c in range(3):
        ext[c, cells_x, cells_y : cells_y + ROWS, :] = jnp.broadcast_to(
            ebuf[c, 0:1, :], (ROWS, wide)
        )

    def strain_plane(x):
        gx, gy, gz = [], [], []
        rows = cells_y + ROWS

        def next_z(a):
            return pltpu.roll(a, wide - 1, 1)[:, :cells_z]

        def next_y(a):
            return pltpu.roll(a, rows - 1, 0)[:cells_y]

        for c in range(3):
            low, high = ext[c, x], ext[c, x + 1]
            diff, both = high - low, high + low
            diff = diff[:, :cells_z] + next_z(diff)
            moved = next_z(both)
            both = both[:, :cells_z]
            both, dz = both + moved, moved - both
            moved = next_y(both)
            gx.append(0.25 * (diff[:cells_y] + next_y(diff)))
            gy.append(0.25 * (moved - both[:cells_y]))
            gz.append(0.25 * (dz[:cells_y] + next_y(dz)))
        xx = strain0[0] + gx[0]
        yy = strain0[1] + gy[1]
        zz = strain0[2] + gz[2]
        yz = strain0[3] + 0.5 * (gy[2] + gz[1])
        xz = strain0[4] + 0.5 * (gx[2] + gz[0])
        xy = strain0[5] + 0.5 * (gx[1] + gy[0])
        trace = xx + yy + zz
        d1, d2, d3 = xx - yy, yy - zz, zz - xx
        inv = (d1 * d1 + d2 * d2 + d3 * d3) * (1.0 / 6.0) + yz * yz + xz * xz + xy * xy
        masks = phase_masks(lab[x])
        part = pick(masks, tab, T_LATERAL) * trace
        under = part * part + pick(masks, tab, T_FACTOR) * inv
        traw[x] = pick(masks, tab, T_WEIGHT_EQ) * (part + jnp.sqrt(under))
        second[x] = inv

    split = cells_x // 2
    pl.loop(0, split)(strain_plane)

    def put_ay(buf):
        def put(x, rows, value):
            buf[x, pl.ds(rows.start + RADIUS, ROWS), :] = value

        return put

    def first_smoothing(ax, ay, by, bx, copies):
        for copy in copies[:2]:
            copy.wait_recv()
        smooth_x_into(ax, put_ay(ay), cells_x, cells_y)
        sent = halo_y(ay)
        for copy in copies[2:]:
            copy.wait_recv()

        @pl.loop(0, cells_x)
        def _(x):
            bx[x + RADIUS] = smooth_y(by[x])

        return sent + halo_x(bx)

    def second_smoothing(ay, bx, full, copies):
        for copy in copies[:2]:
            copy.wait_recv()

        @pl.loop(0, cells_x)
        def _(x):
            full[x, :, :half] = smooth_y(ay[x])

        for copy in copies[2:]:
            copy.wait_recv()

        def put(x, rows, value):
            full[x, rows, half:] = value

        smooth_x_into(bx, put, cells_x, cells_y)

    w2 = first_smoothing(w_ax, w_ay, w_by, w_bx, w1)
    pl.loop(split, cells_x)(strain_plane)
    tz = halo_z(traw, tl, tr)
    for copy in tz:
        copy.wait_recv()
    step = 8

    @pl.loop(0, cells_x // step)
    def _(i):
        planes = pl.ds(i * step, step)
        out = smooth_z(planes, tl, traw, tr, band_hi, band_lo)
        t_ax[pl.ds(i * step + RADIUS, step)] = out[:, :, :half]
        t_by[planes, RADIUS : RADIUS + cells_y, :] = out[:, :, half:]

    t1 = halo_x(t_ax) + halo_y(t_by)
    second_smoothing(w_ay, w_bx, wfull, w2)
    wz = halo_z(wfull, wl, wr)
    t2 = first_smoothing(t_ax, t_ay, t_by, t_bx, t1)
    for copy in wz:
        copy.wait()
    for copy in tz:
        copy.wait_send()

    @pl.loop(0, cells_x // step)
    def _(i):
        planes = pl.ds(i * step, step)
        wfull[planes] = smooth_z(planes, wl, wfull, wr, band_hi, band_lo)

    load_hist.wait()
    second_smoothing(t_ay, t_bx, traw, t2)

    def finish_plane(x):
        masks = phase_masks(lab[x])
        kappa = jnp.maximum(hist[x], traw[x] / wfull[x])
        start = pick(masks, tab, T_START)
        grown = (
            1.0
            - pick(masks, tab, T_LOSS) / jnp.maximum(kappa, start)
            - pick(masks, tab, T_DUCTILE) * jnp.exp(pick(masks, tab, T_BRITTLE) * (kappa - start))
        )
        damage = jnp.where(kappa > start, grown, 0.0)
        damage_v[x] = damage
        mises_v[x] = (1.0 - damage) * pick(masks, tab, T_STIFF) * jnp.sqrt(second[x])

    stores = []
    for i in range(0, cells_x, step):
        pl.loop(i, i + step)(finish_plane)
        planes = pl.ds(i, step)
        for k, (src, dst) in enumerate(((damage_v, damage_out), (mises_v, mises_out))):
            copy = pltpu.make_async_copy(
                src.at[planes], dst.at[planes], out_sem.at[2 * (i // step) + k]
            )
            copy.start()
            stores.append(copy)
    for copy in stores:
        copy.wait()
    for copy in (node_x, node_y, node_e, node_z, node_zx, node_ze, node_zy) + w1 + w2 + t1 + t2:
        copy.wait_send()


def shards(
    displacement, applied_strain, labels, history,
    modulus, poisson, threshold, ductility, brittleness, weight,
):
    cells_x, cells_y, cells_z = labels.shape
    half = cells_z // 2
    f32 = functools.partial(pltpu.VMEM, dtype=jnp.float32)
    bf16 = functools.partial(pltpu.VMEM, dtype=jnp.bfloat16)
    full = (cells_x, cells_y, cells_z)
    long_x = (cells_x + 2 * RADIUS, cells_y, half)
    long_y = (cells_x, cells_y + 2 * RADIUS, half)
    tile = (cells_x, cells_y, LANES)
    wide = cells_z + LANES
    copies = 27
    scratch = [
        f32((3, cells_x + 1, cells_y + ROWS, wide)),
        f32((3, cells_x, cells_z)),
        f32((3, cells_x, wide)),
        f32((3, ROWS, wide)),
        pltpu.VMEM(full, jnp.int32),
        f32(full), f32(full), f32(full),
        f32((40, cells_z)),
        bf16((cells_z + 2 * LANES, cells_z)), bf16((cells_z + 2 * LANES, cells_z)),
        f32(long_x), f32(long_y), f32(long_y), f32(long_x),
        f32(long_x), f32(long_y), f32(long_y), f32(long_x),
        f32(full), f32(tile), f32(tile), f32(tile), f32(tile), f32(full), f32(full),
        pltpu.SemaphoreType.DMA((3,)),
        pltpu.SemaphoreType.DMA((2 * (cells_x // 8),)),
        pltpu.SemaphoreType.DMA((copies,)),
        pltpu.SemaphoreType.DMA((copies,)),
    ]
    whole = pl.BlockSpec(memory_space=pl.ANY)
    scalars = pl.BlockSpec(memory_space=pltpu.SMEM)
    out = jax.ShapeDtypeStruct(full, jnp.float32)
    return pl.pallas_call(
        kernel,
        out_shape=(out, out),
        in_specs=[whole] * 3 + [scalars] * 7,
        out_specs=(whole, whole),
        scratch_shapes=scratch,
        compiler_params=pltpu.CompilerParams(
            collective_id=0, has_side_effects=True, vmem_limit_bytes=56 * 1024 * 1024
        ),
        name="nonlocal_damage",
    )(
        displacement, labels, history, applied_strain,
        modulus, poisson, threshold, ductility, brittleness, weight,
    )


def solution(mesh):
    block = P("gx", "gy", "gz")
    placed = (P(None, "gx", "gy", "gz"), P(), block, block, P(), P(), P(), P(), P(), P())
    return jax.shard_map(
        shards, mesh=mesh, in_specs=placed, out_specs=(block, block), check_vma=False
    )
```

time: 156 us -> 53.6 us (0.34)
  other arithmetic: 73.4 us -> 0 us
  Pallas kernels: 0 us -> 48.2 us
  waiting for transfers between devices: 44.4 us -> 0 us
  local copies, waits for them, and re-layouts: 20.6 us -> 4.62 us
  starting transfers between devices: 15.4 us -> 0 us
    pallas_call x0 -> x1, Pallas kernels: none -> 48.2 us  [shards(): pl.pallas_call(kernel, out_shape=(out, out), in_specs=[whole] * 3 + [scal...]
    ppermute x9 -> x0, waiting for transfers between devices: 44.4 us -> none  [the longest x3 23 us: padded(): lax.ppermute(tail, axis, [(i, (i + 1) % count) for i in range(count)])]
    add x6 -> x0, other arithmetic: 28.6 us -> none  [the longest x3 26.8 us: smooth_rimmed(): total = term if total is None else total + term]
    mul x3 -> x0, other arithmetic: 21.1 us -> none  [the longest x1 15.6 us: finish(): (1.0 - damage) * stiff / (1.0 + ratio_nu) * jnp.sqrt(3.0 * second_inv)]
    another operation x3 -> x0, other arithmetic: 17 us -> none  [shards(): stacked = jnp.stack([weights_field * equiv_strain, weights_field])]
    ppermute x9 -> x0, starting transfers between devices: 15.4 us -> none  [the longest x3 7.67 us: passed_along(): return lax.ppermute(block, axis, route)]
    slice x13 -> x0, local copies, waits for them, and re-layouts: 10.3 us -> none  [the longest x6 3.95 us: pick_phase(): picked = jnp.where(labels == which_phase, table[which_phase], picked)]
    ppermute x3 -> x0, local copies, waits for them, and re-layouts: 5.74 us -> none  [the longest x1 2.29 us: padded(): lax.ppermute(tail, axis, [(i, (i + 1) % count) for i in range(count)])]
  transfers between devices with their start and end apart: 9 -> 0, of which waited for: 6 -> 0; matrix products, arithmetic and copies ran while one was open for 6% -> 0% of each run, Pallas kernels for 0% -> 0%
where the time goes in v1:
time: 53.6 us; the launch traced here: 53.4 us
  Pallas kernels  48.2 us (90%)
  local copies, waits for them, and re-layouts  4.62 us (9%)
  between operations  0.64 us (1%)
    pallas_call x1, Pallas kernels, shards(): pl.pallas_call(kernel, out_shape=(out, out), in_specs=[whole] * 3 + [scal...  48.2 us
    unnamed x2, local copies, waits for them, and re-layouts  4.62 us

profile of v1, /device:TPU:0, one launch (start us, length us, event | category | flops | bytes accessed | tf_op | source)
XLA Modules:
  0.0 53.4 jit_solution(15161054613295662128)
XLA Ops:
  0.6 48.2 %nonlocal_damage.1 = (f32[32,32,256]{2,1,0:T(8,128)}, f32[32,32,256]{2,1,0:T(8,128)}) custom-call(f32[3,32,32,256]{3,2,1,0:T(8,128)} %disp.1, s32[32,32,256]{2,1,0:T(8,128)} %labels.1, f32[32,32,256]{2,1,0:T(8,128)} %history.1, f32[6]{0:T(128)} %strain0.1, f32[4]{0:T(128)} %modulus.1, f32[4]{0:T(128)} %poisson.1, f32[4]{0:T(128)} %threshold.1, f32[4]{0:T(128)} %ductility.1, ...), custom_call_target="tpu_custom_call" | custom-call | tf_op jit(solution)/shard_map/nonlocal_damage/pallas_call | solution.py:405
  48.8 2.3 %copy.14 = f32[32,32,256]{2,1,0:T(8,128)} copy(f32[32,32,256]{2,1,0:T(8,128)} %get-tuple-element.4) | data formatting | bytes 2097152
  51.1 2.3 %copy.15 = f32[32,32,256]{2,1,0:T(8,128)} copy(f32[32,32,256]{2,1,0:T(8,128)} %get-tuple-element.5) | data formatting | bytes 2097152

commit v2 on v1

v2 whole, which is shorter than its diff:
```python
import functools
import math

import jax
import jax.numpy as jnp
from jax import lax
from jax.experimental import pallas as pl
from jax.experimental.pallas import tpu as pltpu
from jax.sharding import PartitionSpec as P

RADIUS = 8
LANES = 128
ROWS = 8
MESH = pl.DeviceIdType.MESH
TAPS = [math.exp(-2.0 * s * s / (RADIUS * RADIUS)) for s in range(RADIUS + 1)]
T_WEIGHT, T_LATERAL, T_FACTOR, T_WEIGHT_EQ, T_STIFF = range(5)


def phase_masks(labels):
    return (labels == 0, labels == 1, labels == 2)


def pick(masks, tab, which):
    rows = [tab[pl.ds(4 * which + p, 1), : masks[0].shape[-1]] for p in range(4)]
    return jnp.where(
        masks[0], rows[0], jnp.where(masks[1], rows[1], jnp.where(masks[2], rows[2], rows[3]))
    )


def fill_tables(tab, modulus, poisson, weight):
    width = tab.shape[-1]

    def put(which, phase, value):
        tab[4 * which + phase : 4 * which + phase + 1, :] = value

    for p in range(4):
        wide = lambda ref: jnp.full((1, width), ref[p], jnp.float32)
        nu, w = wide(poisson), wide(weight)
        put(T_WEIGHT, p, w)
        put(T_LATERAL, p, 9.0 / (1.0 - 2.0 * nu))
        put(T_FACTOR, p, 120.0 / ((1.0 + nu) * (1.0 + nu)))
        put(T_WEIGHT_EQ, p, w * 0.05)
        put(T_STIFF, p, wide(modulus) / (1.0 + nu) * math.sqrt(3.0))


def fill_bands(band_hi, band_lo):
    depth, width = band_hi.shape

    @pl.loop(0, depth // LANES)
    def _(i):
        rows = pl.ds(pl.multiple_of(i * LANES, LANES), LANES)
        k = lax.broadcasted_iota(jnp.int32, (LANES, width), 0) + i * LANES
        n = lax.broadcasted_iota(jnp.int32, (LANES, width), 1)
        d = (k - LANES - n).astype(jnp.float32)
        g = jnp.where(jnp.abs(d) <= RADIUS, jnp.exp(d * d * (-2.0 / (RADIUS * RADIUS))), 0.0)
        hi = g.astype(jnp.bfloat16)
        band_hi[rows, :] = hi
        band_lo[rows, :] = (g - hi.astype(jnp.float32)).astype(jnp.bfloat16)


def smooth_x_own(src, dst, lanes):
    cells_x, cells_y, _ = src.shape

    @pl.loop(0, cells_y // ROWS)
    def _(j):
        rows = pl.ds(pl.multiple_of(j * ROWS, ROWS), ROWS)
        for first in range(0, cells_x, RADIUS):
            low, high = max(first - RADIUS, 0), min(first + 2 * RADIUS, cells_x)
            col = {x: src[x, rows, lanes] for x in range(low, high)}
            for x in range(first, first + RADIUS):
                total = TAPS[0] * col[x]
                for s in range(1, RADIUS + 1):
                    pair = [col[k] for k in (x - s, x + s) if k in col]
                    if pair:
                        total = total + TAPS[s] * (pair[0] + pair[1] if len(pair) > 1 else pair[0])
                dst[x, rows, lanes] = total


def smooth_x_halo(dst, low, high, lanes):
    cells_x, cells_y, _ = dst.shape

    @pl.loop(0, cells_y // ROWS)
    def _(j):
        rows = pl.ds(pl.multiple_of(j * ROWS, ROWS), ROWS)
        below = [low[k, rows, :] for k in range(RADIUS)]
        above = [high[k, rows, :] for k in range(RADIUS)]
        for i in range(RADIUS):
            total = dst[i, rows, lanes]
            for k in range(i, RADIUS):
                total = total + TAPS[i + RADIUS - k] * below[k]
            dst[i, rows, lanes] = total
            x = cells_x - RADIUS + i
            total = dst[x, rows, lanes]
            for k in range(i + 1):
                total = total + TAPS[RADIUS + k - i] * above[k]
            dst[x, rows, lanes] = total


def smooth_rows(block):
    long = block.shape[0] - ROWS
    cells_y = block.shape[0] - 2 * RADIUS
    total = None
    for r in range(ROWS):
        part = None
        for q in range(3):
            s = ROWS * q + r
            if s > 2 * RADIUS:
                continue
            rows = cells_y if r == 0 else long
            term = TAPS[abs(s - RADIUS)] * block[ROWS * q : ROWS * q + rows]
            part = term if part is None else part + term
        if r:
            part = pltpu.roll(part, long - r, 0)[:cells_y]
        total = part if total is None else total + part
    return total


def smooth_y_own(src, dst, lanes):
    cells_x = src.shape[0]

    @pl.loop(0, cells_x // 2)
    def _(i):
        for k in range(2):
            own = src[2 * i + k, :, lanes]
            edge = jnp.zeros((RADIUS, own.shape[1]), own.dtype)
            dst[2 * i + k, :, lanes] = smooth_rows(jnp.concatenate([edge, own, edge], axis=0))


def smooth_y_halo(dst, low, high, lanes):
    cells_x, cells_y, _ = dst.shape
    group = 8
    row = lax.broadcasted_iota(jnp.int32, (1, RADIUS, low.shape[2]), 1)

    @pl.loop(0, cells_x // group)
    def _(i):
        planes = pl.ds(i * group, group)
        below, above = low[planes], high[planes]
        first = dst[planes, 0:RADIUS, lanes]
        last = dst[planes, cells_y - RADIUS : cells_y, lanes]
        for d in range(RADIUS):
            tap = TAPS[RADIUS - d]
            if d == 0:
                first, last = first + tap * below, last + tap * above
            else:
                first = first + jnp.where(row < RADIUS - d, tap, 0.0) * pltpu.roll(
                    below, RADIUS - d, 1
                )
                last = last + jnp.where(row >= d, tap, 0.0) * pltpu.roll(above, d, 1)
        dst[planes, 0:RADIUS, lanes] = first
        dst[planes, cells_y - RADIUS : cells_y, lanes] = last


def banded(block, band_hi, band_lo):
    planes, cells_y, depth = block.shape
    block = block.reshape(planes * cells_y, depth)
    hi = block.astype(jnp.bfloat16)
    lo = (block - hi.astype(jnp.float32)).astype(jnp.bfloat16)
    dot = functools.partial(jnp.dot, preferred_element_type=jnp.float32)
    out = dot(lo, band_hi) + dot(hi, band_lo) + dot(hi, band_hi)
    return out.reshape(planes, cells_y, out.shape[-1])


def smooth_z_own(src, dst, band_hi, band_lo, group=8):
    own = pl.ds(LANES, src.shape[2])

    @pl.loop(0, src.shape[0] // group)
    def _(i):
        planes = pl.ds(i * group, group)
        dst[planes] = banded(src[planes], band_hi[own, :], band_lo[own, :])


def smooth_z_halo(dst, left, right, band_hi, band_lo, group=8):
    cells_z = dst.shape[2]
    first, last = pl.ds(0, LANES), pl.ds(cells_z - LANES, LANES)
    end = pl.ds(cells_z + LANES, LANES)

    @pl.loop(0, dst.shape[0] // group)
    def _(i):
        planes = pl.ds(i * group, group)
        dst[planes, :, first] += banded(left[planes], band_hi[first, first], band_lo[first, first])
        dst[planes, :, last] += banded(right[planes], band_hi[end, last], band_lo[end, last])


def kernel(
    disp, labels, strain0, modulus, poisson, weight,
    averaged_out, stress_out,
    ext, ysend, ybuf, ebuf, lab, second, tab, band_hi, band_lo,
    w_raw, w_one, w_two, w_z, t_raw, t_z, t_one, t_two,
    w_hx, w_hy, t_hx, t_hy, wl, wr, tl, tr,
    in_sem, out_sem, send_sem, recv_sem,
):
    cells_x, cells_y, cells_z = labels.shape
    half = cells_z // 2
    names = ("gx", "gy", "gz")
    count = {a: lax.axis_size(a) for a in names}
    here = {a: lax.axis_index(a) for a in names}

    def at(**moved):
        return tuple(lax.rem(here[a] + moved.get(a, 0) + count[a], count[a]) for a in names)

    x_up, x_down, y_up, y_down = at(gx=1), at(gx=-1), at(gy=1), at(gy=-1)
    z_up, z_down, d_up, d_down = at(gz=1), at(gz=-1), at(gx=1, gy=1), at(gx=-1, gy=-1)

    barrier = pltpu.get_barrier_semaphore()
    greeted = (x_up, x_down, y_up, y_down, z_up, z_down, d_up, d_down)
    for device in greeted:
        pl.semaphore_signal(barrier, inc=1, device_id=device, device_id_type=MESH)

    load_lab = pltpu.make_async_copy(labels, lab, in_sem.at[0])
    load_disp = pltpu.make_async_copy(
        disp, ext.at[:, pl.ds(0, cells_x), pl.ds(0, cells_y), pl.ds(0, cells_z)], in_sem.at[1]
    )
    load_lab.start()
    load_disp.start()

    slots = iter(range(send_sem.shape[0]))

    def remote(src, dst, device):
        slot = next(slots)
        copy = pltpu.make_async_remote_copy(
            src_ref=src, dst_ref=dst, send_sem=send_sem.at[slot], recv_sem=recv_sem.at[slot],
            device_id=device, device_id_type=MESH,
        )
        copy.start()
        return copy

    lower, upper = pl.ds(0, half), pl.ds(half, half)
    low, high = 0, 1

    def halo_x(buf, lanes, h, phase):
        return (
            remote(buf.at[pl.ds(0, RADIUS), :, lanes], h.at[phase, high], x_down),
            remote(buf.at[pl.ds(cells_x - RADIUS, RADIUS), :, lanes], h.at[phase, low], x_up),
        )

    def halo_y(buf, lanes, h, phase):
        return (
            remote(buf.at[:, pl.ds(0, RADIUS), lanes], h.at[phase, high], y_down),
            remote(buf.at[:, pl.ds(cells_y - RADIUS, RADIUS), lanes], h.at[phase, low], y_up),
        )

    def halo_z(buf, left, right, first, size):
        planes = pl.ds(first, size)
        return (
            remote(buf.at[planes, :, pl.ds(0, LANES)], right.at[planes], z_down),
            remote(buf.at[planes, :, pl.ds(cells_z - LANES, LANES)], left.at[planes], z_up),
        )

    fill_tables(tab, modulus, poisson, weight)
    pl.semaphore_wait(barrier, len(greeted))

    zcols = pl.ds(cells_z, LANES)
    first = pl.ds(0, LANES)
    ys = pl.ds(0, cells_y)
    node_x = remote(disp.at[:, 0], ext.at[:, cells_x, ys, pl.ds(0, cells_z)], x_down)
    node_e = remote(disp.at[:, 0, pl.ds(0, ROWS)], ebuf.at[:, :, pl.ds(0, cells_z)], d_down)
    node_z = remote(
        disp.at[:, :, :, first], ext.at[:, pl.ds(0, cells_x), ys, zcols], z_down
    )
    load_disp.wait()

    @pl.loop(0, cells_x)
    def _(x):
        for c in range(3):
            ysend[c, pl.ds(x, 1), :] = ext[c, x, 0:1, :cells_z]

    node_y = remote(ysend, ybuf.at[:, :, pl.ds(0, cells_z)], y_down)
    load_lab.wait()

    @pl.loop(0, cells_x)
    def _(x):
        w_raw[x] = pick(phase_masks(lab[x]), tab, T_WEIGHT)

    w1 = halo_x(w_raw, lower, w_hx, 0) + halo_y(w_raw, upper, w_hy, 0)
    fill_bands(band_hi, band_lo)
    node_x.wait_recv()
    node_zx = remote(ext.at[:, cells_x, ys, first], ext.at[:, cells_x, ys, zcols], z_down)
    node_e.wait_recv()
    node_ze = remote(ebuf.at[:, :, first], ebuf.at[:, :, zcols], z_down)
    node_y.wait_recv()
    node_zy = remote(ybuf.at[:, :, first], ybuf.at[:, :, zcols], z_down)
    smooth_x_own(w_raw, w_one, lower)
    smooth_y_own(w_raw, w_one, upper)
    for copy in (node_z, node_zx, node_ze, node_zy):
        copy.wait_recv()

    wide = ext.shape[3]

    @pl.loop(0, cells_x)
    def _(x):
        for c in range(3):
            ext[c, x, cells_y : cells_y + ROWS, :] = jnp.broadcast_to(
                ybuf[c, pl.ds(x, 1), :], (ROWS, wide)
            )

    for c in range(3):
        ext[c, cells_x, cells_y : cells_y + ROWS, :] = jnp.broadcast_to(
            ebuf[c, 0:1, :], (ROWS, wide)
        )

    def strain_plane(x):
        gx, gy, gz = [], [], []
        rows = cells_y + ROWS

        def next_z(a):
            return pltpu.roll(a, wide - 1, 1)[:, :cells_z]

        def next_y(a):
            return pltpu.roll(a, rows - 1, 0)[:cells_y]

        for c in range(3):
            low, high = ext[c, x], ext[c, x + 1]
            diff, both = high - low, high + low
            diff = diff[:, :cells_z] + next_z(diff)
            moved = next_z(both)
            both = both[:, :cells_z]
            both, dz = both + moved, moved - both
            moved = next_y(both)
            gx.append(0.25 * (diff[:cells_y] + next_y(diff)))
            gy.append(0.25 * (moved - both[:cells_y]))
            gz.append(0.25 * (dz[:cells_y] + next_y(dz)))
        xx = strain0[0] + gx[0]
        yy = strain0[1] + gy[1]
        zz = strain0[2] + gz[2]
        yz = strain0[3] + 0.5 * (gy[2] + gz[1])
        xz = strain0[4] + 0.5 * (gx[2] + gz[0])
        xy = strain0[5] + 0.5 * (gx[1] + gy[0])
        trace = xx + yy + zz
        d1, d2, d3 = xx - yy, yy - zz, zz - xx
        inv = (d1 * d1 + d2 * d2 + d3 * d3) * (1.0 / 6.0) + yz * yz + xz * xz + xy * xy
        masks = phase_masks(lab[x])
        part = pick(masks, tab, T_LATERAL) * trace
        under = part * part + pick(masks, tab, T_FACTOR) * inv
        t_raw[x] = pick(masks, tab, T_WEIGHT_EQ) * (part + jnp.sqrt(under))
        second[x] = inv

    def wait_recv(copies):
        for copy in copies:
            copy.wait_recv()

    split = cells_x // 2
    pl.loop(0, split)(strain_plane)
    tz = halo_z(t_raw, tl, tr, 0, split)
    wait_recv(w1)
    smooth_x_halo(w_one, w_hx.at[0, low], w_hx.at[0, high], lower)
    w2 = halo_y(w_one, lower, w_hy, 1)
    smooth_y_halo(w_one, w_hy.at[0, low], w_hy.at[0, high], upper)
    w2 += halo_x(w_one, upper, w_hx, 1)
    pl.loop(split, cells_x)(strain_plane)
    tz += halo_z(t_raw, tl, tr, split, cells_x - split)
    smooth_z_own(t_raw, t_z, band_hi, band_lo)
    wait_recv(tz)
    smooth_z_halo(t_z, tl, tr, band_hi, band_lo)
    t1 = halo_x(t_z, lower, t_hx, 0) + halo_y(t_z, upper, t_hy, 0)
    smooth_y_own(w_one, w_two, lower)
    smooth_x_own(w_one, w_two, upper)
    wait_recv(w2)
    smooth_y_halo(w_two, w_hy.at[1, low], w_hy.at[1, high], lower)
    smooth_x_halo(w_two, w_hx.at[1, low], w_hx.at[1, high], upper)
    wz = halo_z(w_two, wl, wr, 0, cells_x)
    smooth_x_own(t_z, t_one, lower)
    smooth_y_own(t_z, t_one, upper)
    wait_recv(t1)
    smooth_x_halo(t_one, t_hx.at[0, low], t_hx.at[0, high], lower)
    t2 = halo_y(t_one, lower, t_hy, 1)
    smooth_y_halo(t_one, t_hy.at[0, low], t_hy.at[0, high], upper)
    t2 += halo_x(t_one, upper, t_hx, 1)

    @pl.loop(0, cells_x)
    def _(x):
        second[x] = pick(phase_masks(lab[x]), tab, T_STIFF) * jnp.sqrt(second[x])

    store_stress = pltpu.make_async_copy(second, stress_out, out_sem.at[0])
    store_stress.start()
    smooth_z_own(w_two, w_z, band_hi, band_lo)
    wait_recv(wz)
    smooth_z_halo(w_z, wl, wr, band_hi, band_lo)
    smooth_y_own(t_one, t_two, lower)
    smooth_x_own(t_one, t_two, upper)

    @pl.loop(0, cells_x)
    def _(x):
        w_z[x] = 1.0 / w_z[x]

    wait_recv(t2)
    smooth_y_halo(t_two, t_hy.at[1, low], t_hy.at[1, high], lower)
    smooth_x_halo(t_two, t_hx.at[1, low], t_hx.at[1, high], upper)

    @pl.loop(0, cells_x)
    def _(x):
        t_two[x] = t_two[x] * w_z[x]

    store = pltpu.make_async_copy(t_two, averaged_out, out_sem.at[1])
    store.start()
    nodes = (node_x, node_y, node_e, node_z, node_zx, node_ze, node_zy)
    for copy in nodes + w1 + w2 + t1 + t2 + tz + wz:
        copy.wait_send()
    store_stress.wait()
    store.wait()


def finish(
    averaged, stress, labels, history, threshold, ductility, brittleness, damage_out, mises_out
):
    masks = phase_masks(labels[...])

    def chosen(ref):
        return jnp.where(
            masks[0], ref[0], jnp.where(masks[1], ref[1], jnp.where(masks[2], ref[2], ref[3]))
        )

    kappa = jnp.maximum(history[...], averaged[...])
    start, ductile, brittle = chosen(threshold), chosen(ductility), chosen(brittleness)
    grown = (
        1.0
        - start * (1.0 - ductile) / jnp.maximum(kappa, start)
        - ductile * jnp.exp(brittle * (start - kappa))
    )
    damage = jnp.where(kappa > start, grown, 0.0)
    damage_out[...] = damage
    mises_out[...] = (1.0 - damage) * stress[...]


def shards(
    displacement, applied_strain, labels, history,
    modulus, poisson, threshold, ductility, brittleness, weight,
):
    cells_x, cells_y, cells_z = labels.shape
    half = cells_z // 2
    f32 = functools.partial(pltpu.VMEM, dtype=jnp.float32)
    bf16 = functools.partial(pltpu.VMEM, dtype=jnp.bfloat16)
    full = (cells_x, cells_y, cells_z)
    tile = (cells_x, cells_y, LANES)
    halo_x = f32((2, 2, RADIUS, cells_y, half))
    halo_y = f32((2, 2, cells_x, RADIUS, half))
    wide = cells_z + LANES
    copies = 29
    scratch = [
        f32((3, cells_x + 1, cells_y + ROWS, wide)),
        f32((3, cells_x, cells_z)),
        f32((3, cells_x, wide)),
        f32((3, ROWS, wide)),
        pltpu.VMEM(full, jnp.int32),
        f32(full),
        f32((24, cells_z)),
        bf16((cells_z + 2 * LANES, cells_z)), bf16((cells_z + 2 * LANES, cells_z)),
        f32(full), f32(full), f32(full), f32(full), f32(full), f32(full), f32(full), f32(full),
        halo_x, halo_y, halo_x, halo_y,
        f32(tile), f32(tile), f32(tile), f32(tile),
        pltpu.SemaphoreType.DMA((2,)),
        pltpu.SemaphoreType.DMA((2,)),
        pltpu.SemaphoreType.DMA((copies,)),
        pltpu.SemaphoreType.DMA((copies,)),
    ]
    whole = pl.BlockSpec(memory_space=pl.ANY)
    scalars = pl.BlockSpec(memory_space=pltpu.SMEM)
    out = jax.ShapeDtypeStruct(full, jnp.float32)
    averaged, stress = pl.pallas_call(
        kernel,
        out_shape=(out, out),
        in_specs=[whole] * 2 + [scalars] * 4,
        out_specs=(whole, whole),
        scratch_shapes=scratch,
        compiler_params=pltpu.CompilerParams(
            collective_id=0, has_side_effects=True, vmem_limit_bytes=40 * 1024 * 1024
        ),
        name="strain_and_average",
    )(displacement, labels, applied_strain, modulus, poisson, weight)
    step = 8
    block = pl.BlockSpec((step, cells_y, cells_z), lambda i: (i, 0, 0))
    return pl.pallas_call(
        finish,
        grid=(cells_x // step,),
        out_shape=(out, out),
        in_specs=[block] * 4 + [scalars] * 3,
        out_specs=(block, block),
        compiler_params=pltpu.CompilerParams(vmem_limit_bytes=8 * 1024 * 1024),
        name="damage_and_stress",
    )(averaged, stress, labels, history, threshold, ductility, brittleness)


def solution(mesh):
    block = P("gx", "gy", "gz")
    placed = (P(None, "gx", "gy", "gz"), P(), block, block, P(), P(), P(), P(), P(), P())
    return jax.shard_map(
        shards, mesh=mesh, in_specs=placed, out_specs=(block, block), check_vma=False
    )
```

time: 53.6 us -> 53.5 us (level)
  Pallas kernels: 48.2 us -> 46.9 us
  local copies, waits for them, and re-layouts: 4.62 us -> 5.74 us
    pallas_call x1 -> x2, Pallas kernels: 48.2 us -> 46.9 us  [the longest x1 43.9 us: shards(): pl.pallas_call(kernel, out_shape=(out, out), in_specs=[whole] * 2 + [scal...]
    unnamed x2 -> x20, local copies, waits for them, and re-layouts: 4.62 us -> 5.74 us
where the time goes in v2:
time: 53.5 us; the launch traced here: 53.3 us
  Pallas kernels  46.9 us (88%)
  local copies, waits for them, and re-layouts  5.74 us (11%)
  between operations  0.69 us (1%)
    pallas_call x1, Pallas kernels, shards(): pl.pallas_call(kernel, out_shape=(out, out), in_specs=[whole] * 2 + [scal...  43.9 us
    unnamed x20, local copies, waits for them, and re-layouts  5.74 us
    pallas_call x1, Pallas kernels, shards(): pl.pallas_call(finish, grid=(cells_x // step,), out_shape=(out, out), in_...  2.96 us

profile of v2, /device:TPU:0, one launch (start us, length us, event | category | flops | bytes accessed | tf_op | source)
XLA Modules:
  0.0 53.3 jit_solution(14527290179662818728)
XLA Ops:
  0.6 0.0 copy-start
  0.6 1.2 %copy-done = s32[32,32,256]{2,1,0:T(8,128)S(1)} copy-done((s32[32,32,256]{2,1,0:T(8,128)S(1)}, s32[32,32,256]{2,1,0:T(8,128)}, u32[]{:S(2)}) %copy-start) | copy-done | bytes 1048600
  1.9 0.0 copy-start.1
  1.9 1.9 %copy-done.1 = f32[3,32,32,256]{3,2,1,0:T(8,128)S(1)} copy-done((f32[3,32,32,256]{3,2,1,0:T(8,128)S(1)}, f32[3,32,32,256]{3,2,1,0:T(8,128)}, u32[]{:S(2)}) %copy-start.1) | copy-done | bytes 3145752
  3.7 0.0 copy-start.6
  3.8 0.7 %copy-done.6 = f32[6]{0:T(128)S(1)} copy-done((f32[6]{0:T(128)S(1)}, f32[6]{0:T(128)}, u32[]{:S(2)}) %copy-start.6) | copy-done | bytes 48
  4.4 0.0 copy-start.7
  4.4 0.7 %copy-done.7 = f32[4]{0:T(128)S(1)} copy-done((f32[4]{0:T(128)S(1)}, f32[4]{0:T(128)}, u32[]{:S(2)}) %copy-start.7) | copy-done | bytes 40
  5.1 0.0 copy-start.8
  5.1 0.7 %copy-done.8 = f32[4]{0:T(128)S(1)} copy-done((f32[4]{0:T(128)S(1)}, f32[4]{0:T(128)}, u32[]{:S(2)}) %copy-start.8) | copy-done | bytes 40
  5.7 0.0 copy-start.9
  5.7 0.7 %copy-done.9 = f32[4]{0:T(128)S(1)} copy-done((f32[4]{0:T(128)S(1)}, f32[4]{0:T(128)}, u32[]{:S(2)}) %copy-start.9) | copy-done | bytes 40
  6.4 0.0 copy-start.2
  6.4 0.0 copy-start.3
  6.4 0.0 copy-start.4
  6.4 0.0 copy-start.5
  6.4 43.9 %strain_and_average.1 = (f32[32,32,256]{2,1,0:T(8,128)S(1)}, f32[32,32,256]{2,1,0:T(8,128)S(1)}) custom-call(f32[3,32,32,256]{3,2,1,0:T(8,128)S(1)} %copy-done.1, s32[32,32,256]{2,1,0:T(8,128)S(1)} %copy-done, f32[6]{0:T(128)S(1)} %copy-done.6, f32[4]{0:T(128)S(1)} %copy-done.7, f32[4]{0:T(128)S(1)} %copy-done.8, f32[4]{0:T(128)S(1)} %copy-done.9), custom_call_target="tpu_custom_call" | custom-call | tf_op jit(solution)/shard_map/strain_and_average/pallas_call | solution.py:458
  50.3 0.0 copy-done.2
  50.3 0.0 copy-done.3
  50.3 0.0 copy-done.4
  50.4 0.0 copy-done.5
  50.4 3.0 %damage_and_stress.1 = (f32[32,32,256]{2,1,0:T(8,128)}, f32[32,32,256]{2,1,0:T(8,128)}) custom-call(f32[32,32,256]{2,1,0:T(8,128)S(1)} %get-tuple-element.4.averaged, f32[32,32,256]{2,1,0:T(8,128)S(1)} %get-tuple-element.5.stress, s32[32,32,256]{2,1,0:T(8,128)S(1)} %copy-done, f32[32,32,256]{2,1,0:T(8,128)S(1)} %copy-done.2, f32[4]{0:T(128)S(1)} %copy-done.3, ...), custom_call_target="tpu_custom_call" | custom-call | tf_op jit(solution)/shard_map/damage_and_stress/pallas_call | solution.py:471
Async XLA Ops:
  0.6 1.2 %copy-start = (s32[32,32,256]{2,1,0:T(8,128)S(1)}, s32[32,32,256]{2,1,0:T(8,128)}, u32[]{:S(2)}) copy-start(s32[32,32,256]{2,1,0:T(8,128)} %labels.3) | copy-start | bytes 3145732
  1.9 1.9 %copy-start.1 = (f32[3,32,32,256]{3,2,1,0:T(8,128)S(1)}, f32[3,32,32,256]{3,2,1,0:T(8,128)}, u32[]{:S(2)}) copy-start(f32[3,32,32,256]{3,2,1,0:T(8,128)} %disp.1) | copy-start | bytes 9437188
  3.7 0.7 %copy-start.6 = (f32[6]{0:T(128)S(1)}, f32[6]{0:T(128)}, u32[]{:S(2)}) copy-start(f32[6]{0:T(128)} %strain0.1) | copy-start | bytes 76
  4.4 0.7 %copy-start.7 = (f32[4]{0:T(128)S(1)}, f32[4]{0:T(128)}, u32[]{:S(2)}) copy-start(f32[4]{0:T(128)} %modulus.1) | copy-start | bytes 52
  5.1 0.7 %copy-start.8 = (f32[4]{0:T(128)S(1)}, f32[4]{0:T(128)}, u32[]{:S(2)}) copy-start(f32[4]{0:T(128)} %poisson.1) | copy-start | bytes 52
  5.7 0.7 %copy-start.9 = (f32[4]{0:T(128)S(1)}, f32[4]{0:T(128)}, u32[]{:S(2)}) copy-start(f32[4]{0:T(128)} %weight.1) | copy-start | bytes 52
  6.4 44.0 %copy-start.2 = (f32[32,32,256]{2,1,0:T(8,128)S(1)}, f32[32,32,256]{2,1,0:T(8,128)}, u32[]{:S(2)}) copy-start(f32[32,32,256]{2,1,0:T(8,128)} %history.1) | copy-start | bytes 3145732
  6.4 44.0 %copy-start.3 = (f32[4]{0:T(128)S(1)}, f32[4]{0:T(128)}, u32[]{:S(2)}) copy-start(f32[4]{0:T(128)} %threshold.1) | copy-start | bytes 52
  6.4 44.0 %copy-start.4 = (f32[4]{0:T(128)S(1)}, f32[4]{0:T(128)}, u32[]{:S(2)}) copy-start(f32[4]{0:T(128)} %ductility.1) | copy-start | bytes 52
  6.4 44.0 %copy-start.5 = (f32[4]{0:T(128)S(1)}, f32[4]{0:T(128)}, u32[]{:S(2)}) copy-start(f32[4]{0:T(128)} %brittleness.1) | copy-start | bytes 52

commit v3 on v2

--- a/solution.py
+++ b/solution.py
@@ -182,8 +182,9 @@
 
 
 def kernel(
-    disp, labels, strain0, modulus, poisson, weight,
+    disp, labels, strain0_in, modulus_in, poisson_in, weight_in,
     averaged_out, stress_out,
+    strain0, modulus, poisson, weight,
     ext, ysend, ybuf, ebuf, lab, second, tab, band_hi, band_lo,
     w_raw, w_one, w_two, w_z, t_raw, t_z, t_one, t_two,
     w_hx, w_hy, t_hx, t_hy, wl, wr, tl, tr,
@@ -210,6 +211,13 @@
     load_disp = pltpu.make_async_copy(
         disp, ext.at[:, pl.ds(0, cells_x), pl.ds(0, cells_y), pl.ds(0, cells_z)], in_sem.at[1]
     )
+    scalars = ((weight_in, weight), (poisson_in, poisson), (modulus_in, modulus),
+               (strain0_in, strain0))
+    load_scalars = [
+        pltpu.make_async_copy(src, dst, in_sem.at[2 + i]) for i, (src, dst) in enumerate(scalars)
+    ]
+    for copy in load_scalars:
+        copy.start()
     load_lab.start()
     load_disp.start()
 
@@ -246,31 +254,33 @@
             remote(buf.at[planes, :, pl.ds(cells_z - LANES, LANES)], left.at[planes], z_up),
         )
 
+    for copy in load_scalars:
+        copy.wait()
     fill_tables(tab, modulus, poisson, weight)
+    load_lab.wait()
+
+    @pl.loop(0, cells_x)
+    def _(x):
+        w_raw[x] = pick(phase_masks(lab[x]), tab, T_WEIGHT)
+
+    load_disp.wait()
+
+    @pl.loop(0, cells_x)
+    def _(x):
+        for c in range(3):
+            ysend[c, pl.ds(x, 1), :] = ext[c, x, 0:1, :cells_z]
+
     pl.semaphore_wait(barrier, len(greeted))
 
     zcols = pl.ds(cells_z, LANES)
     first = pl.ds(0, LANES)
     ys = pl.ds(0, cells_y)
     node_x = remote(disp.at[:, 0], ext.at[:, cells_x, ys, pl.ds(0, cells_z)], x_down)
+    node_y = remote(ysend, ybuf.at[:, :, pl.ds(0, cells_z)], y_down)
     node_e = remote(disp.at[:, 0, pl.ds(0, ROWS)], ebuf.at[:, :, pl.ds(0, cells_z)], d_down)
     node_z = remote(
         disp.at[:, :, :, first], ext.at[:, pl.ds(0, cells_x), ys, zcols], z_down
     )
-    load_disp.wait()
-
-    @pl.loop(0, cells_x)
-    def _(x):
-        for c in range(3):
-            ysend[c, pl.ds(x, 1), :] = ext[c, x, 0:1, :cells_z]
-
-    node_y = remote(ysend, ybuf.at[:, :, pl.ds(0, cells_z)], y_down)
-    load_lab.wait()
-
-    @pl.loop(0, cells_x)
-    def _(x):
-        w_raw[x] = pick(phase_masks(lab[x]), tab, T_WEIGHT)
-
     w1 = halo_x(w_raw, lower, w_hx, 0) + halo_y(w_raw, upper, w_hy, 0)
     fill_bands(band_hi, band_lo)
     node_x.wait_recv()
@@ -341,9 +351,10 @@
     split = cells_x // 2
     pl.loop(0, split)(strain_plane)
     tz = halo_z(t_raw, tl, tr, 0, split)
-    wait_recv(w1)
+    wait_recv(w1[:2])
     smooth_x_halo(w_one, w_hx.at[0, low], w_hx.at[0, high], lower)
     w2 = halo_y(w_one, lower, w_hy, 1)
+    wait_recv(w1[2:])
     smooth_y_halo(w_one, w_hy.at[0, low], w_hy.at[0, high], upper)
     w2 += halo_x(w_one, upper, w_hx, 1)
     pl.loop(split, cells_x)(strain_plane)
@@ -360,9 +371,10 @@
     wz = halo_z(w_two, wl, wr, 0, cells_x)
     smooth_x_own(t_z, t_one, lower)
     smooth_y_own(t_z, t_one, upper)
-    wait_recv(t1)
+    wait_recv(t1[:2])
     smooth_x_halo(t_one, t_hx.at[0, low], t_hx.at[0, high], lower)
     t2 = halo_y(t_one, lower, t_hy, 1)
+    wait_recv(t1[2:])
     smooth_y_halo(t_one, t_hy.at[0, low], t_hy.at[0, high], upper)
     t2 += halo_x(t_one, upper, t_hx, 1)
 
@@ -435,7 +447,9 @@
     halo_y = f32((2, 2, cells_x, RADIUS, half))
     wide = cells_z + LANES
     copies = 29
+    smem = functools.partial(pltpu.SMEM, dtype=jnp.float32)
     scratch = [
+        smem(applied_strain.shape), smem(modulus.shape), smem(poisson.shape), smem(weight.shape),
         f32((3, cells_x + 1, cells_y + ROWS, wide)),
         f32((3, cells_x, cells_z)),
         f32((3, cells_x, wide)),
@@ -447,7 +461,7 @@
         f32(full), f32(full), f32(full), f32(full), f32(full), f32(full), f32(full), f32(full),
         halo_x, halo_y, halo_x, halo_y,
         f32(tile), f32(tile), f32(tile), f32(tile),
-        pltpu.SemaphoreType.DMA((2,)),
+        pltpu.SemaphoreType.DMA((6,)),
         pltpu.SemaphoreType.DMA((2,)),
         pltpu.SemaphoreType.DMA((copies,)),
         pltpu.SemaphoreType.DMA((copies,)),
@@ -458,11 +472,11 @@
     averaged, stress = pl.pallas_call(
         kernel,
         out_shape=(out, out),
-        in_specs=[whole] * 2 + [scalars] * 4,
+        in_specs=[pl.BlockSpec(memory_space=pltpu.HBM)] * 6,
         out_specs=(whole, whole),
         scratch_shapes=scratch,
         compiler_params=pltpu.CompilerParams(
-            collective_id=0, has_side_effects=True, vmem_limit_bytes=40 * 1024 * 1024
+            collective_id=0, has_side_effects=True, vmem_limit_bytes=56 * 1024 * 1024
         ),
         name="strain_and_average",
     )(displacement, labels, applied_strain, modulus, poisson, weight)
@@ -474,7 +488,7 @@
         out_shape=(out, out),
         in_specs=[block] * 4 + [scalars] * 3,
         out_specs=(block, block),
-        compiler_params=pltpu.CompilerParams(vmem_limit_bytes=8 * 1024 * 1024),
+        compiler_params=pltpu.CompilerParams(vmem_limit_bytes=56 * 1024 * 1024),
         name="damage_and_stress",
     )(averaged, stress, labels, history, threshold, ductility, brittleness)
 

time: 53.5 us -> 49.8 us (0.931)
  local copies, waits for them, and re-layouts: 5.74 us -> 0 us
  Pallas kernels: 46.9 us -> 48.9 us
    unnamed x20 -> x0, local copies, waits for them, and re-layouts: 5.74 us -> none
    pallas_call x1, Pallas kernels: 2.96 us -> 4.58 us  [shards(): pl.pallas_call(finish, grid=(cells_x // step,), out_shape=(out, out), in_...]
where the time goes in v3:
time: 49.8 us; the launch traced here: 49.6 us
  Pallas kernels  48.9 us (98%)
  between operations  0.64 us (1%)
    pallas_call x1, Pallas kernels, shards(): pl.pallas_call(kernel, out_shape=(out, out), in_specs=[pl.BlockSpec(memor...  44.3 us
    pallas_call x1, Pallas kernels, shards(): pl.pallas_call(finish, grid=(cells_x // step,), out_shape=(out, out), in_...  4.58 us

profile of v3, /device:TPU:0, one launch (start us, length us, event | category | flops | bytes accessed | tf_op | source)
XLA Modules:
  0.0 49.6 jit_solution(13154142250359159021)
XLA Ops:
  0.6 44.3 %strain_and_average.1 = (f32[32,32,256]{2,1,0:T(8,128)}, f32[32,32,256]{2,1,0:T(8,128)}) custom-call(f32[3,32,32,256]{3,2,1,0:T(8,128)} %disp.1, s32[32,32,256]{2,1,0:T(8,128)} %labels.3, f32[6]{0:T(128)} %strain0_in.1, f32[4]{0:T(128)} %modulus_in.1, f32[4]{0:T(128)} %poisson_in.1, f32[4]{0:T(128)} %weight_in.1), custom_call_target="tpu_custom_call" | custom-call | tf_op jit(solution)/shard_map/strain_and_average/pallas_call | solution.py:472
  45.0 4.6 %damage_and_stress.1 = (f32[32,32,256]{2,1,0:T(8,128)}, f32[32,32,256]{2,1,0:T(8,128)}) custom-call(f32[32,32,256]{2,1,0:T(8,128)} %get-tuple-element.4.averaged, f32[32,32,256]{2,1,0:T(8,128)} %get-tuple-element.5.stress, s32[32,32,256]{2,1,0:T(8,128)} %labels.3, f32[32,32,256]{2,1,0:T(8,128)} %history.1, f32[4]{0:T(128)} %threshold.1, f32[4]{0:T(128)} %ductility.1, ...), custom_call_target="tpu_custom_call" | custom-call | tf_op jit(solution)/shard_map/damage_and_stress/pallas_call | solution.py:485

commit v4 on v3

--- a/solution.py
+++ b/solution.py
@@ -76,11 +76,14 @@
                 dst[x, rows, lanes] = total
 
 
-def smooth_x_halo(dst, low, high, lanes):
+def ends_and_middle(count):
+    return ((0, 1), (count - 1, count)), ((1, count - 1),)
+
+
+def smooth_x_halo(dst, low, high, lanes, spans):
     cells_x, cells_y, _ = dst.shape
 
-    @pl.loop(0, cells_y // ROWS)
-    def _(j):
+    def step(j):
         rows = pl.ds(pl.multiple_of(j * ROWS, ROWS), ROWS)
         below = [low[k, rows, :] for k in range(RADIUS)]
         above = [high[k, rows, :] for k in range(RADIUS)]
@@ -94,6 +97,9 @@
             for k in range(i + 1):
                 total = total + TAPS[RADIUS + k - i] * above[k]
             dst[x, rows, lanes] = total
+
+    for span in spans:
+        pl.loop(*span)(step)
 
 
 def smooth_rows(block):
@@ -126,13 +132,12 @@
             dst[2 * i + k, :, lanes] = smooth_rows(jnp.concatenate([edge, own, edge], axis=0))
 
 
-def smooth_y_halo(dst, low, high, lanes):
+def smooth_y_halo(dst, low, high, lanes, spans):
     cells_x, cells_y, _ = dst.shape
     group = 8
     row = lax.broadcasted_iota(jnp.int32, (1, RADIUS, low.shape[2]), 1)
 
-    @pl.loop(0, cells_x // group)
-    def _(i):
+    def step(i):
         planes = pl.ds(i * group, group)
         below, above = low[planes], high[planes]
         first = dst[planes, 0:RADIUS, lanes]
@@ -149,6 +154,9 @@
         dst[planes, 0:RADIUS, lanes] = first
         dst[planes, cells_y - RADIUS : cells_y, lanes] = last
 
+    for span in spans:
+        pl.loop(*span)(step)
+
 
 def banded(block, band_hi, band_lo):
     planes, cells_y, depth = block.shape
@@ -182,10 +190,10 @@
 
 
 def kernel(
-    disp, labels, strain0_in, modulus_in, poisson_in, weight_in,
-    averaged_out, stress_out,
+    disp, labels, history, strain0_in, modulus_in, poisson_in, weight_in,
+    kappa_out, stress_out,
     strain0, modulus, poisson, weight,
-    ext, ysend, ybuf, ebuf, lab, second, tab, band_hi, band_lo,
+    ext, edge, ysend, ybuf, ebuf, lab, hist, second, tab, band_hi, band_lo,
     w_raw, w_one, w_two, w_z, t_raw, t_z, t_one, t_two,
     w_hx, w_hy, t_hx, t_hy, wl, wr, tl, tr,
     in_sem, out_sem, send_sem, recv_sem,
@@ -218,8 +226,10 @@
     ]
     for copy in load_scalars:
         copy.start()
-    load_lab.start()
-    load_disp.start()
+    load_edge = pltpu.make_async_copy(disp.at[:, :, pl.ds(0, ROWS)], edge, in_sem.at[6])
+    load_hist = pltpu.make_async_copy(history, hist, in_sem.at[7])
+    for copy in (load_edge, load_lab, load_disp, load_hist):
+        copy.start()
 
     slots = iter(range(send_sem.shape[0]))
 
@@ -254,33 +264,32 @@
             remote(buf.at[planes, :, pl.ds(cells_z - LANES, LANES)], left.at[planes], z_up),
         )
 
-    for copy in load_scalars:
-        copy.wait()
-    fill_tables(tab, modulus, poisson, weight)
-    load_lab.wait()
-
-    @pl.loop(0, cells_x)
-    def _(x):
-        w_raw[x] = pick(phase_masks(lab[x]), tab, T_WEIGHT)
-
-    load_disp.wait()
+    load_edge.wait()
 
     @pl.loop(0, cells_x)
     def _(x):
         for c in range(3):
-            ysend[c, pl.ds(x, 1), :] = ext[c, x, 0:1, :cells_z]
-
-    pl.semaphore_wait(barrier, len(greeted))
+            ysend[c, pl.ds(x, 1), :] = edge[c, x, 0:1, :]
 
     zcols = pl.ds(cells_z, LANES)
     first = pl.ds(0, LANES)
     ys = pl.ds(0, cells_y)
+    pl.semaphore_wait(barrier, len(greeted))
     node_x = remote(disp.at[:, 0], ext.at[:, cells_x, ys, pl.ds(0, cells_z)], x_down)
     node_y = remote(ysend, ybuf.at[:, :, pl.ds(0, cells_z)], y_down)
     node_e = remote(disp.at[:, 0, pl.ds(0, ROWS)], ebuf.at[:, :, pl.ds(0, cells_z)], d_down)
     node_z = remote(
         disp.at[:, :, :, first], ext.at[:, pl.ds(0, cells_x), ys, zcols], z_down
     )
+    for copy in load_scalars:
+        copy.wait()
+    fill_tables(tab, modulus, poisson, weight)
+    load_lab.wait()
+
+    @pl.loop(0, cells_x)
+    def _(x):
+        w_raw[x] = pick(phase_masks(lab[x]), tab, T_WEIGHT)
+
     w1 = halo_x(w_raw, lower, w_hx, 0) + halo_y(w_raw, upper, w_hy, 0)
     fill_bands(band_hi, band_lo)
     node_x.wait_recv()
@@ -295,6 +304,7 @@
         copy.wait_recv()
 
     wide = ext.shape[3]
+    load_disp.wait()
 
     @pl.loop(0, cells_x)
     def _(x):
@@ -344,6 +354,9 @@
         t_raw[x] = pick(masks, tab, T_WEIGHT_EQ) * (part + jnp.sqrt(under))
         second[x] = inv
 
+    row_ends, row_middle = ends_and_middle(cells_y // ROWS)
+    plane_ends, plane_middle = ends_and_middle(cells_x // 8)
+
     def wait_recv(copies):
         for copy in copies:
             copy.wait_recv()
@@ -352,11 +365,13 @@
     pl.loop(0, split)(strain_plane)
     tz = halo_z(t_raw, tl, tr, 0, split)
     wait_recv(w1[:2])
-    smooth_x_halo(w_one, w_hx.at[0, low], w_hx.at[0, high], lower)
+    smooth_x_halo(w_one, w_hx.at[0, low], w_hx.at[0, high], lower, row_ends)
     w2 = halo_y(w_one, lower, w_hy, 1)
     wait_recv(w1[2:])
-    smooth_y_halo(w_one, w_hy.at[0, low], w_hy.at[0, high], upper)
+    smooth_y_halo(w_one, w_hy.at[0, low], w_hy.at[0, high], upper, plane_ends)
     w2 += halo_x(w_one, upper, w_hx, 1)
+    smooth_x_halo(w_one, w_hx.at[0, low], w_hx.at[0, high], lower, row_middle)
+    smooth_y_halo(w_one, w_hy.at[0, low], w_hy.at[0, high], upper, plane_middle)
     pl.loop(split, cells_x)(strain_plane)
     tz += halo_z(t_raw, tl, tr, split, cells_x - split)
     smooth_z_own(t_raw, t_z, band_hi, band_lo)
@@ -366,17 +381,19 @@
     smooth_y_own(w_one, w_two, lower)
     smooth_x_own(w_one, w_two, upper)
     wait_recv(w2)
-    smooth_y_halo(w_two, w_hy.at[1, low], w_hy.at[1, high], lower)
-    smooth_x_halo(w_two, w_hx.at[1, low], w_hx.at[1, high], upper)
+    smooth_y_halo(w_two, w_hy.at[1, low], w_hy.at[1, high], lower, plane_ends + plane_middle)
+    smooth_x_halo(w_two, w_hx.at[1, low], w_hx.at[1, high], upper, row_ends + row_middle)
     wz = halo_z(w_two, wl, wr, 0, cells_x)
     smooth_x_own(t_z, t_one, lower)
     smooth_y_own(t_z, t_one, upper)
     wait_recv(t1[:2])
-    smooth_x_halo(t_one, t_hx.at[0, low], t_hx.at[0, high], lower)
+    smooth_x_halo(t_one, t_hx.at[0, low], t_hx.at[0, high], lower, row_ends)
     t2 = halo_y(t_one, lower, t_hy, 1)
     wait_recv(t1[2:])
-    smooth_y_halo(t_one, t_hy.at[0, low], t_hy.at[0, high], upper)
+    smooth_y_halo(t_one, t_hy.at[0, low], t_hy.at[0, high], upper, plane_ends)
     t2 += halo_x(t_one, upper, t_hx, 1)
+    smooth_x_halo(t_one, t_hx.at[0, low], t_hx.at[0, high], lower, row_middle)
+    smooth_y_halo(t_one, t_hy.at[0, low], t_hy.at[0, high], upper, plane_middle)
 
     @pl.loop(0, cells_x)
     def _(x):
@@ -394,43 +411,85 @@
     def _(x):
         w_z[x] = 1.0 / w_z[x]
 
-    wait_recv(t2)
-    smooth_y_halo(t_two, t_hy.at[1, low], t_hy.at[1, high], lower)
-    smooth_x_halo(t_two, t_hx.at[1, low], t_hx.at[1, high], upper)
-
-    @pl.loop(0, cells_x)
-    def _(x):
-        t_two[x] = t_two[x] * w_z[x]
-
-    store = pltpu.make_async_copy(t_two, averaged_out, out_sem.at[1])
-    store.start()
+    load_hist.wait()
+    wait_recv(t2[:2])
+    smooth_y_halo(
+        t_two, t_hy.at[1, low], t_hy.at[1, high], lower, plane_ends + plane_middle
+    )
+    stores = []
+
+    def largest(x):
+        hist[x] = jnp.maximum(hist[x], t_two[x] * w_z[x])
+
+    def store_planes(start):
+        pl.loop(start, start + RADIUS)(largest)
+        planes = pl.ds(start, RADIUS)
+        copy = pltpu.make_async_copy(
+            hist.at[planes], kappa_out.at[planes], out_sem.at[1 + start // RADIUS]
+        )
+        copy.start()
+        stores.append(copy)
+
+    for start in range(RADIUS, cells_x - RADIUS, RADIUS):
+        store_planes(start)
+    wait_recv(t2[2:])
+    smooth_x_halo(t_two, t_hx.at[1, low], t_hx.at[1, high], upper, row_ends + row_middle)
+    for start in (0, cells_x - RADIUS):
+        store_planes(start)
     nodes = (node_x, node_y, node_e, node_z, node_zx, node_ze, node_zy)
     for copy in nodes + w1 + w2 + t1 + t2 + tz + wz:
         copy.wait_send()
-    store_stress.wait()
-    store.wait()
+    for copy in [store_stress] + stores:
+        copy.wait()
 
 
 def finish(
-    averaged, stress, labels, history, threshold, ductility, brittleness, damage_out, mises_out
+    kappa_in, stress_in, labels_in, threshold, ductility, brittleness, damage_out, mises_out,
+    kappa, stress, labels, damage, mises, in_sem, out_sem, *, step,
 ):
-    masks = phase_masks(labels[...])
-
-    def chosen(ref):
-        return jnp.where(
-            masks[0], ref[0], jnp.where(masks[1], ref[1], jnp.where(masks[2], ref[2], ref[3]))
-        )
-
-    kappa = jnp.maximum(history[...], averaged[...])
-    start, ductile, brittle = chosen(threshold), chosen(ductility), chosen(brittleness)
-    grown = (
-        1.0
-        - start * (1.0 - ductile) / jnp.maximum(kappa, start)
-        - ductile * jnp.exp(brittle * (start - kappa))
-    )
-    damage = jnp.where(kappa > start, grown, 0.0)
-    damage_out[...] = damage
-    mises_out[...] = (1.0 - damage) * stress[...]
+    cells_x = labels.shape[0]
+    chunks = range(0, cells_x, step)
+    pairs = ((kappa_in, kappa), (labels_in, labels), (stress_in, stress))
+    loads, stores = [], []
+    for i, start in enumerate(chunks):
+        planes = pl.ds(start, step)
+        loads.append([
+            pltpu.make_async_copy(src.at[planes], dst.at[planes], in_sem.at[3 * i + k])
+            for k, (src, dst) in enumerate(pairs)
+        ])
+        for copy in loads[-1]:
+            copy.start()
+
+    def plane(x):
+        masks = phase_masks(labels[x])
+
+        def chosen(ref):
+            return jnp.where(
+                masks[0], ref[0], jnp.where(masks[1], ref[1], jnp.where(masks[2], ref[2], ref[3]))
+            )
+
+        start, ductile, brittle = chosen(threshold), chosen(ductility), chosen(brittleness)
+        now = kappa[x]
+        grown = (
+            1.0
+            - start * (1.0 - ductile) / jnp.maximum(now, start)
+            - ductile * jnp.exp(brittle * (start - now))
+        )
+        grown = jnp.where(now > start, grown, 0.0)
+        damage[x] = grown
+        mises[x] = (1.0 - grown) * stress[x]
+
+    for i, start in enumerate(chunks):
+        for copy in loads[i]:
+            copy.wait()
+        pl.loop(start, start + step)(plane)
+        planes = pl.ds(start, step)
+        for k, (src, dst) in enumerate(((damage, damage_out), (mises, mises_out))):
+            copy = pltpu.make_async_copy(src.at[planes], dst.at[planes], out_sem.at[2 * i + k])
+            copy.start()
+            stores.append(copy)
+    for copy in stores:
+        copy.wait()
 
 
 def shards(
@@ -451,46 +510,51 @@
     scratch = [
         smem(applied_strain.shape), smem(modulus.shape), smem(poisson.shape), smem(weight.shape),
         f32((3, cells_x + 1, cells_y + ROWS, wide)),
+        f32((3, cells_x, ROWS, cells_z)),
         f32((3, cells_x, cells_z)),
         f32((3, cells_x, wide)),
         f32((3, ROWS, wide)),
         pltpu.VMEM(full, jnp.int32),
-        f32(full),
+        f32(full), f32(full),
         f32((24, cells_z)),
         bf16((cells_z + 2 * LANES, cells_z)), bf16((cells_z + 2 * LANES, cells_z)),
         f32(full), f32(full), f32(full), f32(full), f32(full), f32(full), f32(full), f32(full),
         halo_x, halo_y, halo_x, halo_y,
         f32(tile), f32(tile), f32(tile), f32(tile),
-        pltpu.SemaphoreType.DMA((6,)),
-        pltpu.SemaphoreType.DMA((2,)),
+        pltpu.SemaphoreType.DMA((8,)),
+        pltpu.SemaphoreType.DMA((1 + cells_x // RADIUS,)),
         pltpu.SemaphoreType.DMA((copies,)),
         pltpu.SemaphoreType.DMA((copies,)),
     ]
     whole = pl.BlockSpec(memory_space=pl.ANY)
     scalars = pl.BlockSpec(memory_space=pltpu.SMEM)
     out = jax.ShapeDtypeStruct(full, jnp.float32)
-    averaged, stress = pl.pallas_call(
+    kappa, stress = pl.pallas_call(
         kernel,
         out_shape=(out, out),
-        in_specs=[pl.BlockSpec(memory_space=pltpu.HBM)] * 6,
+        in_specs=[whole] * 7,
         out_specs=(whole, whole),
         scratch_shapes=scratch,
         compiler_params=pltpu.CompilerParams(
             collective_id=0, has_side_effects=True, vmem_limit_bytes=56 * 1024 * 1024
         ),
         name="strain_and_average",
-    )(displacement, labels, applied_strain, modulus, poisson, weight)
+    )(displacement, labels, history, applied_strain, modulus, poisson, weight)
     step = 8
-    block = pl.BlockSpec((step, cells_y, cells_z), lambda i: (i, 0, 0))
+    chunks = cells_x // step
     return pl.pallas_call(
-        finish,
-        grid=(cells_x // step,),
+        functools.partial(finish, step=step),
         out_shape=(out, out),
-        in_specs=[block] * 4 + [scalars] * 3,
-        out_specs=(block, block),
+        in_specs=[whole] * 3 + [scalars] * 3,
+        out_specs=(whole, whole),
+        scratch_shapes=[
+            f32(full), f32(full), pltpu.VMEM(full, jnp.int32), f32(full), f32(full),
+            pltpu.SemaphoreType.DMA((3 * chunks,)),
+            pltpu.SemaphoreType.DMA((2 * chunks,)),
+        ],
         compiler_params=pltpu.CompilerParams(vmem_limit_bytes=56 * 1024 * 1024),
         name="damage_and_stress",
-    )(averaged, stress, labels, history, threshold, ductility, brittleness)
+    )(kappa, stress, labels, threshold, ductility, brittleness)
 
 
 def solution(mesh):

time: 49.8 us -> 48.9 us (0.982)
  Pallas kernels: 48.9 us -> 48.1 us
    pallas_call x2, Pallas kernels: 48.9 us -> 48.1 us  [the longest x1 44 us: shards(): pl.pallas_call(kernel, out_shape=(out, out), in_specs=[whole] * 7, out_sp...]
where the time goes in v4:
time: 48.9 us; the launch traced here: 48.8 us
  Pallas kernels  48.1 us (98%)
  between operations  0.64 us (1%)
    pallas_call x1, Pallas kernels, shards(): pl.pallas_call(kernel, out_shape=(out, out), in_specs=[whole] * 7, out_sp...  44 us
    pallas_call x1, Pallas kernels, shards(): pl.pallas_call(functools.partial(finish, step=step), out_shape=(out, out)...  4.14 us

profile of v4, /device:TPU:0, one launch (start us, length us, event | category | flops | bytes accessed | tf_op | source)
XLA Modules:
  0.0 48.8 jit_solution(6605710177842245941)
XLA Ops:
  0.6 44.0 %strain_and_average.1 = (f32[32,32,256]{2,1,0:T(8,128)}, f32[32,32,256]{2,1,0:T(8,128)}) custom-call(f32[3,32,32,256]{3,2,1,0:T(8,128)} %disp.1, s32[32,32,256]{2,1,0:T(8,128)} %labels_in.1, f32[32,32,256]{2,1,0:T(8,128)} %history.1, f32[6]{0:T(128)} %strain0_in.1, f32[4]{0:T(128)} %modulus_in.1, f32[4]{0:T(128)} %poisson_in.1, f32[4]{0:T(128)} %weight_in.1), custom_call_target="tpu_custom_call" | custom-call | tf_op jit(solution)/shard_map/strain_and_average/pallas_call | solution.py:532
  44.6 4.1 %damage_and_stress.1 = (f32[32,32,256]{2,1,0:T(8,128)}, f32[32,32,256]{2,1,0:T(8,128)}) custom-call(f32[32,32,256]{2,1,0:T(8,128)} %get-tuple-element.4.kappa_in, f32[32,32,256]{2,1,0:T(8,128)} %get-tuple-element.5.stress_in, s32[32,32,256]{2,1,0:T(8,128)} %labels_in.1, f32[4]{0:T(128)} %threshold.1, f32[4]{0:T(128)} %ductility.1, f32[4]{0:T(128)} %brittleness.1), custom_call_target="tpu_custom_call" | custom-call | tf_op jit(solution)/shard_map/damage_and_stress/pallas_call | solution.py:545

commit v5 on v4

--- a/solution.py
+++ b/solution.py
@@ -13,7 +13,7 @@
 ROWS = 8
 MESH = pl.DeviceIdType.MESH
 TAPS = [math.exp(-2.0 * s * s / (RADIUS * RADIUS)) for s in range(RADIUS + 1)]
-T_WEIGHT, T_LATERAL, T_FACTOR, T_WEIGHT_EQ, T_STIFF = range(5)
+T_WEIGHT, T_LATERAL, T_FACTOR, T_STIFF = range(4)
 
 
 def phase_masks(labels):
@@ -37,10 +37,10 @@
         wide = lambda ref: jnp.full((1, width), ref[p], jnp.float32)
         nu, w = wide(poisson), wide(weight)
         put(T_WEIGHT, p, w)
-        put(T_LATERAL, p, 9.0 / (1.0 - 2.0 * nu))
-        put(T_FACTOR, p, 120.0 / ((1.0 + nu) * (1.0 + nu)))
-        put(T_WEIGHT_EQ, p, w * 0.05)
-        put(T_STIFF, p, wide(modulus) / (1.0 + nu) * math.sqrt(3.0))
+        scaled = w * (1.0 / 80.0)
+        put(T_LATERAL, p, scaled * 9.0 / (1.0 - 2.0 * nu))
+        put(T_FACTOR, p, scaled * scaled * 120.0 / ((1.0 + nu) * (1.0 + nu)))
+        put(T_STIFF, p, wide(modulus) / (1.0 + nu) * (0.25 * math.sqrt(3.0)))
 
 
 def fill_bands(band_hi, band_lo):
@@ -193,7 +193,7 @@
     disp, labels, history, strain0_in, modulus_in, poisson_in, weight_in,
     kappa_out, stress_out,
     strain0, modulus, poisson, weight,
-    ext, edge, ysend, ybuf, ebuf, lab, hist, second, tab, band_hi, band_lo,
+    ext, sums, edge, ysend, ybuf, ebuf, lab, hist, second, tab, band_hi, band_lo,
     w_raw, w_one, w_two, w_z, t_raw, t_z, t_one, t_two,
     w_hx, w_hy, t_hx, t_hy, wl, wr, tl, tr,
     in_sem, out_sem, send_sem, recv_sem,
@@ -318,41 +318,44 @@
             ebuf[c, 0:1, :], (ROWS, wide)
         )
 
+    rows = cells_y + ROWS
+
+    def node_sums(c, x):
+        plane = ext[c, x]
+        moved = pltpu.roll(plane, wide - 1, 1)[:, :cells_z]
+        plane = plane[:, :cells_z]
+        both, diff = moved + plane, moved - plane
+        next_both = pltpu.roll(both, rows - 1, 0)[:cells_y]
+        next_diff = pltpu.roll(diff, rows - 1, 0)[:cells_y]
+        both, diff = both[:cells_y], diff[:cells_y]
+        return both + next_both, next_both - both, diff + next_diff
+
     def strain_plane(x):
         gx, gy, gz = [], [], []
-        rows = cells_y + ROWS
-
-        def next_z(a):
-            return pltpu.roll(a, wide - 1, 1)[:, :cells_z]
-
-        def next_y(a):
-            return pltpu.roll(a, rows - 1, 0)[:cells_y]
-
         for c in range(3):
-            low, high = ext[c, x], ext[c, x + 1]
-            diff, both = high - low, high + low
-            diff = diff[:, :cells_z] + next_z(diff)
-            moved = next_z(both)
-            both = both[:, :cells_z]
-            both, dz = both + moved, moved - both
-            moved = next_y(both)
-            gx.append(0.25 * (diff[:cells_y] + next_y(diff)))
-            gy.append(0.25 * (moved - both[:cells_y]))
-            gz.append(0.25 * (dz[:cells_y] + next_y(dz)))
-        xx = strain0[0] + gx[0]
-        yy = strain0[1] + gy[1]
-        zz = strain0[2] + gz[2]
-        yz = strain0[3] + 0.5 * (gy[2] + gz[1])
-        xz = strain0[4] + 0.5 * (gx[2] + gz[0])
-        xy = strain0[5] + 0.5 * (gx[1] + gy[0])
+            new = node_sums(c, x + 1)
+            gx.append(new[0] - sums[3 * c])
+            gy.append(new[1] + sums[3 * c + 1])
+            gz.append(new[2] + sums[3 * c + 2])
+            for k in range(3):
+                sums[3 * c + k] = new[k]
+        xx = 4.0 * strain0[0] + gx[0]
+        yy = 4.0 * strain0[1] + gy[1]
+        zz = 4.0 * strain0[2] + gz[2]
+        yz = 8.0 * strain0[3] + (gy[2] + gz[1])
+        xz = 8.0 * strain0[4] + (gx[2] + gz[0])
+        xy = 8.0 * strain0[5] + (gx[1] + gy[0])
         trace = xx + yy + zz
         d1, d2, d3 = xx - yy, yy - zz, zz - xx
-        inv = (d1 * d1 + d2 * d2 + d3 * d3) * (1.0 / 6.0) + yz * yz + xz * xz + xy * xy
+        inv = (d1 * d1 + d2 * d2 + d3 * d3) * (1.0 / 6.0) + 0.25 * (yz * yz + xz * xz + xy * xy)
         masks = phase_masks(lab[x])
         part = pick(masks, tab, T_LATERAL) * trace
-        under = part * part + pick(masks, tab, T_FACTOR) * inv
-        t_raw[x] = pick(masks, tab, T_WEIGHT_EQ) * (part + jnp.sqrt(under))
+        t_raw[x] = part + jnp.sqrt(part * part + pick(masks, tab, T_FACTOR) * inv)
         second[x] = inv
+
+    for c in range(3):
+        for k, value in enumerate(node_sums(c, 0)):
+            sums[3 * c + k] = value
 
     row_ends, row_middle = ends_and_middle(cells_y // ROWS)
     plane_ends, plane_middle = ends_and_middle(cells_x // 8)
@@ -510,13 +513,14 @@
     scratch = [
         smem(applied_strain.shape), smem(modulus.shape), smem(poisson.shape), smem(weight.shape),
         f32((3, cells_x + 1, cells_y + ROWS, wide)),
+        f32((9, cells_y, cells_z)),
         f32((3, cells_x, ROWS, cells_z)),
         f32((3, cells_x, cells_z)),
         f32((3, cells_x, wide)),
         f32((3, ROWS, wide)),
         pltpu.VMEM(full, jnp.int32),
         f32(full), f32(full),
-        f32((24, cells_z)),
+        f32((16, cells_z)),
         bf16((cells_z + 2 * LANES, cells_z)), bf16((cells_z + 2 * LANES, cells_z)),
         f32(full), f32(full), f32(full), f32(full), f32(full), f32(full), f32(full), f32(full),
         halo_x, halo_y, halo_x, halo_y,

time: 48.9 us -> 48.2 us (0.986)
  Pallas kernels: 48.1 us -> 47.4 us
    pallas_call x1, Pallas kernels: 44 us -> 43.3 us  [shards(): pl.pallas_call(kernel, out_shape=(out, out), in_specs=[whole] * 7, out_sp...]
where the time goes in v5:
time: 48.2 us; the launch traced here: 48 us
  Pallas kernels  47.4 us (98%)
  between operations  0.64 us (1%)
    pallas_call x1, Pallas kernels, shards(): pl.pallas_call(kernel, out_shape=(out, out), in_specs=[whole] * 7, out_sp...  43.3 us
    pallas_call x1, Pallas kernels, shards(): pl.pallas_call(functools.partial(finish, step=step), out_shape=(out, out)...  4.14 us

profile of v5, /device:TPU:0, one launch (start us, length us, event | category | flops | bytes accessed | tf_op | source)
XLA Modules:
  0.0 48.0 jit_solution(7928685878480129151)
XLA Ops:
  0.6 43.3 %strain_and_average.1 = (f32[32,32,256]{2,1,0:T(8,128)}, f32[32,32,256]{2,1,0:T(8,128)}) custom-call(f32[3,32,32,256]{3,2,1,0:T(8,128)} %disp.1, s32[32,32,256]{2,1,0:T(8,128)} %labels_in.1, f32[32,32,256]{2,1,0:T(8,128)} %history.1, f32[6]{0:T(128)} %strain0_in.1, f32[4]{0:T(128)} %modulus_in.1, f32[4]{0:T(128)} %poisson_in.1, f32[4]{0:T(128)} %weight_in.1), custom_call_target="tpu_custom_call" | custom-call | tf_op jit(solution)/shard_map/strain_and_average/pallas_call | solution.py:536
  43.9 4.1 %damage_and_stress.1 = (f32[32,32,256]{2,1,0:T(8,128)}, f32[32,32,256]{2,1,0:T(8,128)}) custom-call(f32[32,32,256]{2,1,0:T(8,128)} %get-tuple-element.4.kappa_in, f32[32,32,256]{2,1,0:T(8,128)} %get-tuple-element.5.stress_in, s32[32,32,256]{2,1,0:T(8,128)} %labels_in.1, f32[4]{0:T(128)} %threshold.1, f32[4]{0:T(128)} %ductility.1, f32[4]{0:T(128)} %brittleness.1), custom_call_target="tpu_custom_call" | custom-call | tf_op jit(solution)/shard_map/damage_and_stress/pallas_call | solution.py:549

commit v6 on v5

--- a/solution.py
+++ b/solution.py
@@ -177,16 +177,42 @@
         dst[planes] = banded(src[planes], band_hi[own, :], band_lo[own, :])
 
 
-def smooth_z_halo(dst, left, right, band_hi, band_lo, group=8):
-    cells_z = dst.shape[2]
+def pack_z(src, ends):
+    cells_x, cells_y, cells_z = src.shape
+    per = LANES // RADIUS
+    column = lax.broadcasted_iota(jnp.int32, (cells_y, LANES), 1)
+    for i in range(pl.cdiv(cells_x, per)):
+        tiles = [jnp.zeros((cells_y, LANES), jnp.float32)] * 2
+        for p in range(min(per, cells_x - i * per)):
+            x = i * per + p
+            here = (column >= p * RADIUS) & (column < (p + 1) * RADIUS)
+            first, last = src[x, :, 0:LANES], src[x, :, cells_z - LANES : cells_z]
+            if p:
+                first = pltpu.roll(first, p * RADIUS, 1)
+            if p < per - 1:
+                last = pltpu.roll(last, (p + 1) * RADIUS, 1)
+            tiles = [jnp.where(here, first, tiles[0]), jnp.where(here, last, tiles[1])]
+        ends[0, i], ends[1, i] = tiles
+
+
+def smooth_z_halo(dst, left, right, band_hi, band_lo):
+    cells_x, _, cells_z = dst.shape
+    per = LANES // RADIUS
     first, last = pl.ds(0, LANES), pl.ds(cells_z - LANES, LANES)
     end = pl.ds(cells_z + LANES, LANES)
-
-    @pl.loop(0, dst.shape[0] // group)
-    def _(i):
-        planes = pl.ds(i * group, group)
-        dst[planes, :, first] += banded(left[planes], band_hi[first, first], band_lo[first, first])
-        dst[planes, :, last] += banded(right[planes], band_hi[end, last], band_lo[end, last])
+    group = 8
+    for start in range(0, cells_x, group):
+        lefts, rights = [], []
+        for x in range(start, start + group):
+            i, p = divmod(x, per)
+            low, high = left[i], right[i]
+            lefts.append(pltpu.roll(low, LANES - (p + 1) * RADIUS, 1) if p < per - 1 else low)
+            rights.append(pltpu.roll(high, LANES - p * RADIUS, 1) if p else high)
+        planes = pl.ds(start, group)
+        dst[planes, :, first] += banded(
+            jnp.stack(lefts), band_hi[first, first], band_lo[first, first]
+        )
+        dst[planes, :, last] += banded(jnp.stack(rights), band_hi[end, last], band_lo[end, last])
 
 
 def kernel(
@@ -195,7 +221,7 @@
     strain0, modulus, poisson, weight,
     ext, sums, edge, ysend, ybuf, ebuf, lab, hist, second, tab, band_hi, band_lo,
     w_raw, w_one, w_two, w_z, t_raw, t_z, t_one, t_two,
-    w_hx, w_hy, t_hx, t_hy, wl, wr, tl, tr,
+    w_hx, w_hy, t_hx, t_hy, w_sx, w_sy, t_sx, t_sy, w_ends, t_ends, wl, wr, tl, tr,
     in_sem, out_sem, send_sem, recv_sem,
 ):
     cells_x, cells_y, cells_z = labels.shape
@@ -245,24 +271,21 @@
     lower, upper = pl.ds(0, half), pl.ds(half, half)
     low, high = 0, 1
 
-    def halo_x(buf, lanes, h, phase):
-        return (
-            remote(buf.at[pl.ds(0, RADIUS), :, lanes], h.at[phase, high], x_down),
-            remote(buf.at[pl.ds(cells_x - RADIUS, RADIUS), :, lanes], h.at[phase, low], x_up),
-        )
-
-    def halo_y(buf, lanes, h, phase):
-        return (
-            remote(buf.at[:, pl.ds(0, RADIUS), lanes], h.at[phase, high], y_down),
-            remote(buf.at[:, pl.ds(cells_y - RADIUS, RADIUS), lanes], h.at[phase, low], y_up),
-        )
-
-    def halo_z(buf, left, right, first, size):
-        planes = pl.ds(first, size)
-        return (
-            remote(buf.at[planes, :, pl.ds(0, LANES)], right.at[planes], z_down),
-            remote(buf.at[planes, :, pl.ds(cells_z - LANES, LANES)], left.at[planes], z_up),
-        )
+    def halo_x(buf, lanes, h, phase, sent):
+        sent[phase, low] = buf[0:RADIUS, :, lanes]
+        down = remote(sent.at[phase, low], h.at[phase, high], x_down)
+        sent[phase, high] = buf[cells_x - RADIUS : cells_x, :, lanes]
+        return down, remote(sent.at[phase, high], h.at[phase, low], x_up)
+
+    def halo_y(buf, lanes, h, phase, sent):
+        sent[phase, low] = buf[:, 0:RADIUS, lanes]
+        down = remote(sent.at[phase, low], h.at[phase, high], y_down)
+        sent[phase, high] = buf[:, cells_y - RADIUS : cells_y, lanes]
+        return down, remote(sent.at[phase, high], h.at[phase, low], y_up)
+
+    def halo_z(buf, ends, left, right):
+        pack_z(buf, ends)
+        return remote(ends.at[0], right, z_down), remote(ends.at[1], left, z_up)
 
     load_edge.wait()
 
@@ -290,7 +313,7 @@
     def _(x):
         w_raw[x] = pick(phase_masks(lab[x]), tab, T_WEIGHT)
 
-    w1 = halo_x(w_raw, lower, w_hx, 0) + halo_y(w_raw, upper, w_hy, 0)
+    w1 = halo_x(w_raw, lower, w_hx, 0, w_sx) + halo_y(w_raw, upper, w_hy, 0, w_sy)
     fill_bands(band_hi, band_lo)
     node_x.wait_recv()
     node_zx = remote(ext.at[:, cells_x, ys, first], ext.at[:, cells_x, ys, zcols], z_down)
@@ -364,37 +387,36 @@
         for copy in copies:
             copy.wait_recv()
 
-    split = cells_x // 2
+    split = 3 * cells_x // 8
     pl.loop(0, split)(strain_plane)
-    tz = halo_z(t_raw, tl, tr, 0, split)
     wait_recv(w1[:2])
     smooth_x_halo(w_one, w_hx.at[0, low], w_hx.at[0, high], lower, row_ends)
-    w2 = halo_y(w_one, lower, w_hy, 1)
+    w2 = halo_y(w_one, lower, w_hy, 1, w_sy)
     wait_recv(w1[2:])
     smooth_y_halo(w_one, w_hy.at[0, low], w_hy.at[0, high], upper, plane_ends)
-    w2 += halo_x(w_one, upper, w_hx, 1)
+    w2 += halo_x(w_one, upper, w_hx, 1, w_sx)
     smooth_x_halo(w_one, w_hx.at[0, low], w_hx.at[0, high], lower, row_middle)
     smooth_y_halo(w_one, w_hy.at[0, low], w_hy.at[0, high], upper, plane_middle)
     pl.loop(split, cells_x)(strain_plane)
-    tz += halo_z(t_raw, tl, tr, split, cells_x - split)
+    tz = halo_z(t_raw, t_ends, tl, tr)
     smooth_z_own(t_raw, t_z, band_hi, band_lo)
     wait_recv(tz)
     smooth_z_halo(t_z, tl, tr, band_hi, band_lo)
-    t1 = halo_x(t_z, lower, t_hx, 0) + halo_y(t_z, upper, t_hy, 0)
+    t1 = halo_x(t_z, lower, t_hx, 0, t_sx) + halo_y(t_z, upper, t_hy, 0, t_sy)
     smooth_y_own(w_one, w_two, lower)
     smooth_x_own(w_one, w_two, upper)
     wait_recv(w2)
     smooth_y_halo(w_two, w_hy.at[1, low], w_hy.at[1, high], lower, plane_ends + plane_middle)
     smooth_x_halo(w_two, w_hx.at[1, low], w_hx.at[1, high], upper, row_ends + row_middle)
-    wz = halo_z(w_two, wl, wr, 0, cells_x)
+    wz = halo_z(w_two, w_ends, wl, wr)
     smooth_x_own(t_z, t_one, lower)
     smooth_y_own(t_z, t_one, upper)
     wait_recv(t1[:2])
     smooth_x_halo(t_one, t_hx.at[0, low], t_hx.at[0, high], lower, row_ends)
-    t2 = halo_y(t_one, lower, t_hy, 1)
+    t2 = halo_y(t_one, lower, t_hy, 1, t_sy)
     wait_recv(t1[2:])
     smooth_y_halo(t_one, t_hy.at[0, low], t_hy.at[0, high], upper, plane_ends)
-    t2 += halo_x(t_one, upper, t_hx, 1)
+    t2 += halo_x(t_one, upper, t_hx, 1, t_sx)
     smooth_x_halo(t_one, t_hx.at[0, low], t_hx.at[0, high], lower, row_middle)
     smooth_y_halo(t_one, t_hy.at[0, low], t_hy.at[0, high], upper, plane_middle)
 
@@ -504,11 +526,11 @@
     f32 = functools.partial(pltpu.VMEM, dtype=jnp.float32)
     bf16 = functools.partial(pltpu.VMEM, dtype=jnp.bfloat16)
     full = (cells_x, cells_y, cells_z)
-    tile = (cells_x, cells_y, LANES)
+    tile = (pl.cdiv(cells_x * RADIUS, LANES), cells_y, LANES)
     halo_x = f32((2, 2, RADIUS, cells_y, half))
     halo_y = f32((2, 2, cells_x, RADIUS, half))
     wide = cells_z + LANES
-    copies = 29
+    copies = 27
     smem = functools.partial(pltpu.SMEM, dtype=jnp.float32)
     scratch = [
         smem(applied_strain.shape), smem(modulus.shape), smem(poisson.shape), smem(weight.shape),
@@ -523,7 +545,8 @@
         f32((16, cells_z)),
         bf16((cells_z + 2 * LANES, cells_z)), bf16((cells_z + 2 * LANES, cells_z)),
         f32(full), f32(full), f32(full), f32(full), f32(full), f32(full), f32(full), f32(full),
-        halo_x, halo_y, halo_x, halo_y,
+        halo_x, halo_y, halo_x, halo_y, halo_x, halo_y, halo_x, halo_y,
+        f32((2,) + tile), f32((2,) + tile),
         f32(tile), f32(tile), f32(tile), f32(tile),
         pltpu.SemaphoreType.DMA((8,)),
         pltpu.SemaphoreType.DMA((1 + cells_x // RADIUS,)),

time: 48.2 us -> 47.3 us (0.981)
  Pallas kernels: 47.4 us -> 46.5 us
    pallas_call x1, Pallas kernels: 43.3 us -> 42.3 us  [shards(): pl.pallas_call(kernel, out_shape=(out, out), in_specs=[whole] * 7, out_sp...]
where the time goes in v6:
time: 47.3 us; the launch traced here: 47.1 us
  Pallas kernels  46.5 us (98%)
  between operations  0.64 us (1%)
    pallas_call x1, Pallas kernels, shards(): pl.pallas_call(kernel, out_shape=(out, out), in_specs=[whole] * 7, out_sp...  42.3 us
    pallas_call x1, Pallas kernels, shards(): pl.pallas_call(functools.partial(finish, step=step), out_shape=(out, out)...  4.14 us

profile of v6, /device:TPU:0, one launch (start us, length us, event | category | flops | bytes accessed | tf_op | source)
XLA Modules:
  0.0 47.1 jit_solution(17475773368431821150)
XLA Ops:
  0.6 42.3 %strain_and_average.1 = (f32[32,32,256]{2,1,0:T(8,128)}, f32[32,32,256]{2,1,0:T(8,128)}) custom-call(f32[3,32,32,256]{3,2,1,0:T(8,128)} %disp.1, s32[32,32,256]{2,1,0:T(8,128)} %labels_in.1, f32[32,32,256]{2,1,0:T(8,128)} %history.1, f32[6]{0:T(128)} %strain0_in.1, f32[4]{0:T(128)} %modulus_in.1, f32[4]{0:T(128)} %poisson_in.1, f32[4]{0:T(128)} %weight_in.1), custom_call_target="tpu_custom_call" | custom-call | tf_op jit(solution)/shard_map/strain_and_average/pallas_call | solution.py:559
  43.0 4.1 %damage_and_stress.1 = (f32[32,32,256]{2,1,0:T(8,128)}, f32[32,32,256]{2,1,0:T(8,128)}) custom-call(f32[32,32,256]{2,1,0:T(8,128)} %get-tuple-element.4.kappa_in, f32[32,32,256]{2,1,0:T(8,128)} %get-tuple-element.5.stress_in, s32[32,32,256]{2,1,0:T(8,128)} %labels_in.1, f32[4]{0:T(128)} %threshold.1, f32[4]{0:T(128)} %ductility.1, f32[4]{0:T(128)} %brittleness.1), custom_call_target="tpu_custom_call" | custom-call | tf_op jit(solution)/shard_map/damage_and_stress/pallas_call | solution.py:572

commit v7 on v6

--- a/solution.py
+++ b/solution.py
@@ -77,16 +77,17 @@
 
 
 def ends_and_middle(count):
-    return ((0, 1), (count - 1, count)), ((1, count - 1),)
+    return ((0, 1, 0), (count - 1, count, 2 - count)), ((1, count - 1, 1),)
 
 
 def smooth_x_halo(dst, low, high, lanes, spans):
     cells_x, cells_y, _ = dst.shape
 
-    def step(j):
+    def step(j, offset):
         rows = pl.ds(pl.multiple_of(j * ROWS, ROWS), ROWS)
-        below = [low[k, rows, :] for k in range(RADIUS)]
-        above = [high[k, rows, :] for k in range(RADIUS)]
+        held = pl.ds(pl.multiple_of((j + offset) * ROWS, ROWS), ROWS)
+        below = [low[k, held, :] for k in range(RADIUS)]
+        above = [high[k, held, :] for k in range(RADIUS)]
         for i in range(RADIUS):
             total = dst[i, rows, lanes]
             for k in range(i, RADIUS):
@@ -98,8 +99,8 @@
                 total = total + TAPS[RADIUS + k - i] * above[k]
             dst[x, rows, lanes] = total
 
-    for span in spans:
-        pl.loop(*span)(step)
+    for start, stop, offset in spans:
+        pl.loop(start, stop)(functools.partial(step, offset=offset))
 
 
 def smooth_rows(block):
@@ -137,9 +138,10 @@
     group = 8
     row = lax.broadcasted_iota(jnp.int32, (1, RADIUS, low.shape[2]), 1)
 
-    def step(i):
+    def step(i, offset):
         planes = pl.ds(i * group, group)
-        below, above = low[planes], high[planes]
+        held = pl.ds((i + offset) * group, group)
+        below, above = low[held], high[held]
         first = dst[planes, 0:RADIUS, lanes]
         last = dst[planes, cells_y - RADIUS : cells_y, lanes]
         for d in range(RADIUS):
@@ -154,8 +156,8 @@
         dst[planes, 0:RADIUS, lanes] = first
         dst[planes, cells_y - RADIUS : cells_y, lanes] = last
 
-    for span in spans:
-        pl.loop(*span)(step)
+    for start, stop, offset in spans:
+        pl.loop(start, stop)(functools.partial(step, offset=offset))
 
 
 def banded(block, band_hi, band_lo):
@@ -271,17 +273,58 @@
     lower, upper = pl.ds(0, half), pl.ds(half, half)
     low, high = 0, 1
 
-    def halo_x(buf, lanes, h, phase, sent):
-        sent[phase, low] = buf[0:RADIUS, :, lanes]
-        down = remote(sent.at[phase, low], h.at[phase, high], x_down)
-        sent[phase, high] = buf[cells_x - RADIUS : cells_x, :, lanes]
-        return down, remote(sent.at[phase, high], h.at[phase, low], x_up)
-
-    def halo_y(buf, lanes, h, phase, sent):
-        sent[phase, low] = buf[:, 0:RADIUS, lanes]
-        down = remote(sent.at[phase, low], h.at[phase, high], y_down)
-        sent[phase, high] = buf[:, cells_y - RADIUS : cells_y, lanes]
-        return down, remote(sent.at[phase, high], h.at[phase, low], y_up)
+    row_ends, row_middle = ends_and_middle(cells_y // ROWS)
+    plane_ends, plane_middle = ends_and_middle(cells_x // 8)
+
+    def wait_recv(copies):
+        for copy in copies:
+            copy.wait_recv()
+
+    ends_first = lambda size: (
+        (pl.ds(0, RADIUS), pl.ds(0, RADIUS)),
+        (pl.ds(RADIUS, RADIUS), pl.ds(size - RADIUS, RADIUS)),
+        (pl.ds(2 * RADIUS, size - 2 * RADIUS), pl.ds(RADIUS, size - 2 * RADIUS)),
+    )
+
+    def halo_x(buf, lanes, h, phase, sent, rest):
+        for to, of in ends_first(cells_y)[2:] if rest else ends_first(cells_y)[:2]:
+            sent[phase, low, :, to, :] = buf[0:RADIUS, of, lanes]
+            sent[phase, high, :, to, :] = buf[cells_x - RADIUS : cells_x, of, lanes]
+        part = pl.ds(2 * RADIUS, cells_y - 2 * RADIUS) if rest else pl.ds(0, 2 * RADIUS)
+        return (
+            remote(sent.at[phase, low, :, part], h.at[phase, high, :, part], x_down),
+            remote(sent.at[phase, high, :, part], h.at[phase, low, :, part], x_up),
+        )
+
+    def halo_y(buf, lanes, h, phase, sent, rest):
+        for to, of in ends_first(cells_x)[2:] if rest else ends_first(cells_x)[:2]:
+            sent[phase, low, to] = buf[of, 0:RADIUS, lanes]
+            sent[phase, high, to] = buf[of, cells_y - RADIUS : cells_y, lanes]
+        part = pl.ds(2 * RADIUS, cells_x - 2 * RADIUS) if rest else pl.ds(0, 2 * RADIUS)
+        return (
+            remote(sent.at[phase, low, part], h.at[phase, high, part], y_down),
+            remote(sent.at[phase, high, part], h.at[phase, low, part], y_up),
+        )
+
+    def first_halos(buf, hx, hy, sx, sy):
+        sent = ()
+        for rest in (False, True):
+            sent += halo_x(buf, lower, hx, 0, sx, rest) + halo_y(buf, upper, hy, 0, sy, rest)
+        return sent
+
+    def second_halos(one, first, hx, hy, sx, sy):
+        from_x, from_y = (hx.at[0, low], hx.at[0, high]), (hy.at[0, low], hy.at[0, high])
+        wait_recv(first[0:2])
+        smooth_x_halo(one, *from_x, lower, row_ends)
+        along_y = halo_y(one, lower, hy, 1, sy, False) + halo_y(one, lower, hy, 1, sy, True)
+        wait_recv(first[2:4])
+        smooth_y_halo(one, *from_y, upper, plane_ends)
+        along_x = halo_x(one, upper, hx, 1, sx, False) + halo_x(one, upper, hx, 1, sx, True)
+        wait_recv(first[4:6])
+        smooth_x_halo(one, *from_x, lower, row_middle)
+        wait_recv(first[6:8])
+        smooth_y_halo(one, *from_y, upper, plane_middle)
+        return along_y + along_x
 
     def halo_z(buf, ends, left, right):
         pack_z(buf, ends)
@@ -313,7 +356,7 @@
     def _(x):
         w_raw[x] = pick(phase_masks(lab[x]), tab, T_WEIGHT)
 
-    w1 = halo_x(w_raw, lower, w_hx, 0, w_sx) + halo_y(w_raw, upper, w_hy, 0, w_sy)
+    w1 = first_halos(w_raw, w_hx, w_hy, w_sx, w_sy)
     fill_bands(band_hi, band_lo)
     node_x.wait_recv()
     node_zx = remote(ext.at[:, cells_x, ys, first], ext.at[:, cells_x, ys, zcols], z_down)
@@ -380,29 +423,15 @@
         for k, value in enumerate(node_sums(c, 0)):
             sums[3 * c + k] = value
 
-    row_ends, row_middle = ends_and_middle(cells_y // ROWS)
-    plane_ends, plane_middle = ends_and_middle(cells_x // 8)
-
-    def wait_recv(copies):
-        for copy in copies:
-            copy.wait_recv()
-
     split = 3 * cells_x // 8
     pl.loop(0, split)(strain_plane)
-    wait_recv(w1[:2])
-    smooth_x_halo(w_one, w_hx.at[0, low], w_hx.at[0, high], lower, row_ends)
-    w2 = halo_y(w_one, lower, w_hy, 1, w_sy)
-    wait_recv(w1[2:])
-    smooth_y_halo(w_one, w_hy.at[0, low], w_hy.at[0, high], upper, plane_ends)
-    w2 += halo_x(w_one, upper, w_hx, 1, w_sx)
-    smooth_x_halo(w_one, w_hx.at[0, low], w_hx.at[0, high], lower, row_middle)
-    smooth_y_halo(w_one, w_hy.at[0, low], w_hy.at[0, high], upper, plane_middle)
+    w2 = second_halos(w_one, w1, w_hx, w_hy, w_sx, w_sy)
     pl.loop(split, cells_x)(strain_plane)
     tz = halo_z(t_raw, t_ends, tl, tr)
     smooth_z_own(t_raw, t_z, band_hi, band_lo)
     wait_recv(tz)
     smooth_z_halo(t_z, tl, tr, band_hi, band_lo)
-    t1 = halo_x(t_z, lower, t_hx, 0, t_sx) + halo_y(t_z, upper, t_hy, 0, t_sy)
+    t1 = first_halos(t_z, t_hx, t_hy, t_sx, t_sy)
     smooth_y_own(w_one, w_two, lower)
     smooth_x_own(w_one, w_two, upper)
     wait_recv(w2)
@@ -411,14 +440,7 @@
     wz = halo_z(w_two, w_ends, wl, wr)
     smooth_x_own(t_z, t_one, lower)
     smooth_y_own(t_z, t_one, upper)
-    wait_recv(t1[:2])
-    smooth_x_halo(t_one, t_hx.at[0, low], t_hx.at[0, high], lower, row_ends)
-    t2 = halo_y(t_one, lower, t_hy, 1, t_sy)
-    wait_recv(t1[2:])
-    smooth_y_halo(t_one, t_hy.at[0, low], t_hy.at[0, high], upper, plane_ends)
-    t2 += halo_x(t_one, upper, t_hx, 1, t_sx)
-    smooth_x_halo(t_one, t_hx.at[0, low], t_hx.at[0, high], lower, row_middle)
-    smooth_y_halo(t_one, t_hy.at[0, low], t_hy.at[0, high], upper, plane_middle)
+    t2 = second_halos(t_one, t1, t_hx, t_hy, t_sx, t_sy)
 
     @pl.loop(0, cells_x)
     def _(x):
@@ -437,7 +459,7 @@
         w_z[x] = 1.0 / w_z[x]
 
     load_hist.wait()
-    wait_recv(t2[:2])
+    wait_recv(t2[:4])
     smooth_y_halo(
         t_two, t_hy.at[1, low], t_hy.at[1, high], lower, plane_ends + plane_middle
     )
@@ -457,7 +479,7 @@
 
     for start in range(RADIUS, cells_x - RADIUS, RADIUS):
         store_planes(start)
-    wait_recv(t2[2:])
+    wait_recv(t2[4:])
     smooth_x_halo(t_two, t_hx.at[1, low], t_hx.at[1, high], upper, row_ends + row_middle)
     for start in (0, cells_x - RADIUS):
         store_planes(start)
@@ -530,7 +552,7 @@
     halo_x = f32((2, 2, RADIUS, cells_y, half))
     halo_y = f32((2, 2, cells_x, RADIUS, half))
     wide = cells_z + LANES
-    copies = 27
+    copies = 43
     smem = functools.partial(pltpu.SMEM, dtype=jnp.float32)
     scratch = [
         smem(applied_strain.shape), smem(modulus.shape), smem(poisson.shape), smem(weight.shape),

time: 47.3 us -> 44.6 us (0.943)
  Pallas kernels: 46.5 us -> 43.8 us
    pallas_call x1, Pallas kernels: 42.3 us -> 39.7 us  [shards(): pl.pallas_call(kernel, out_shape=(out, out), in_specs=[whole] * 7, out_sp...]
where the time goes in v7:
time: 44.6 us; the launch traced here: 44.5 us
  Pallas kernels  43.8 us (98%)
  between operations  0.64 us (1%)
    pallas_call x1, Pallas kernels, shards(): pl.pallas_call(kernel, out_shape=(out, out), in_specs=[whole] * 7, out_sp...  39.7 us
    pallas_call x1, Pallas kernels, shards(): pl.pallas_call(functools.partial(finish, step=step), out_shape=(out, out)...  4.14 us

profile of v7, /device:TPU:0, one launch (start us, length us, event | category | flops | bytes accessed | tf_op | source)
XLA Modules:
  0.0 44.5 jit_solution(6128477845975434361)
XLA Ops:
  0.6 39.7 %strain_and_average.1 = (f32[32,32,256]{2,1,0:T(8,128)}, f32[32,32,256]{2,1,0:T(8,128)}) custom-call(f32[3,32,32,256]{3,2,1,0:T(8,128)} %disp.1, s32[32,32,256]{2,1,0:T(8,128)} %labels_in.1, f32[32,32,256]{2,1,0:T(8,128)} %history.1, f32[6]{0:T(128)} %strain0_in.1, f32[4]{0:T(128)} %modulus_in.1, f32[4]{0:T(128)} %poisson_in.1, f32[4]{0:T(128)} %weight_in.1), custom_call_target="tpu_custom_call" | custom-call | tf_op jit(solution)/shard_map/strain_and_average/pallas_call | solution.py:581
  40.3 4.1 %damage_and_stress.1 = (f32[32,32,256]{2,1,0:T(8,128)}, f32[32,32,256]{2,1,0:T(8,128)}) custom-call(f32[32,32,256]{2,1,0:T(8,128)} %get-tuple-element.4.kappa_in, f32[32,32,256]{2,1,0:T(8,128)} %get-tuple-element.5.stress_in, s32[32,32,256]{2,1,0:T(8,128)} %labels_in.1, f32[4]{0:T(128)} %threshold.1, f32[4]{0:T(128)} %ductility.1, f32[4]{0:T(128)} %brittleness.1), custom_call_target="tpu_custom_call" | custom-call | tf_op jit(solution)/shard_map/damage_and_stress/pallas_call | solution.py:594
